TPU v7x, 256 devices: a whole 4x4x8 slice. The times are simulated.
256 devices in a mesh: dp: 32 (over y_lo, z, core), ctx: 8 (over y_hi, x).
Axes of the slice: x: 4, y: 4 (y_hi: 2, y_lo: 2; y = y_hi * 2 + y_lo), z: 8, core: 2. Of those that a mesh axis runs over, the one named last changes fastest.
Arguments:
- queries: bfloat16 [32, 1024, 4096], P('dp', 'ctx'), may hold values from -5 to 5
- key_vectors: bfloat16 [32, 1024, 512], P('dp', 'ctx'), may hold values from -5 to 5
- activations: bfloat16 [32, 1024, 4096], P('dp', 'ctx'), may hold values from -6 to 6
- value_weight: bfloat16 [4096, 512], P(('dp', 'ctx')), may hold values from -0.09375 to 0.09375
- attended_grad: bfloat16 [32, 1024, 4096], P('dp', 'ctx'), may hold values from -6 to 6
- doc_ids: int32 [32, 1024], P('dp'), may hold values from 0 to 15, never falling along the last dimension, each value on 1 to 512 neighbouring positions
- shard_plan: int32 [32, 32], P('dp'), may hold values from 0 to 31, as said below
- round_bits: int32 [8, 1024, 8], replicated, may hold values from 0 to 1073741823
Outputs:
- attended: bfloat16 [32, 1024, 4096], P('dp', 'ctx')
- query_grad: bfloat16 [32, 1024, 4096], P('dp', 'ctx')
- key_grad: bfloat16 [32, 1024, 512], P('dp', 'ctx')
- weight_grad: float32 [4096, 512], P(('dp', 'ctx'))
Inputs may be any that keep to these rules, and one draw needn't show every extreme that they name: Each row is a permutation of the 32 blocks; index d of ctx holds the places of blocks shard_plan[s, d * 4] to shard_plan[s, d * 4 + 3] in this order, and of these at most 1 come from any one index of ctx (block b comes from index b // 4), a bound reached in every row.
All inputs are finite; a program needn't handle non-finite values.
Results may differ from a plain program's by a relative error of at most 0.022.
Values may be sent and summed in bfloat16 or wider, within the bound.
A program may use at most 192 MiB of HBM per device.

v0:
```python
import jax
import jax.numpy as jnp
from jax import lax
from jax.sharding import PartitionSpec as P

HEADS = 32
KV_HEADS = 4
HEAD_DIM = 128
BPD = 4


def shifted(x, axis, by):
    devices = lax.axis_size(axis)
    return lax.ppermute(x, axis, [(i, (i + by) % devices) for i in range(devices)])


def block_maps(plan_row, device_index, cycle_size, per_device, capacity):
    total_blocks = plan_row.shape[0]
    blocks = jnp.arange(total_blocks, dtype=jnp.int32)
    matches = (plan_row[:, None] == blocks[None, :]).astype(jnp.int32)
    place_of = jnp.sum(matches * blocks[:, None], axis=0)
    target = place_of // per_device
    owners = blocks // per_device
    within = blocks % per_device
    earlier = (
        (owners[:, None] == owners[None, :])
        & (within[None, :] < within[:, None])
        & (target[:, None] == target[None, :])
    )
    ranking = jnp.sum(earlier.astype(jnp.int32), axis=1)
    send_slot = lax.dynamic_slice_in_dim(
        target * capacity + ranking, device_index * per_device, per_device
    )
    held_blocks = lax.dynamic_slice_in_dim(plan_row, device_index * per_device, per_device)
    from_slot = jnp.take(owners * capacity + ranking, held_blocks)
    slot_ids = jnp.arange(cycle_size * capacity, dtype=jnp.int32)
    packing = (slot_ids[:, None] == send_slot[None, :]).astype(jnp.bfloat16)
    unpacking = (from_slot[:, None] == slot_ids[None, :]).astype(jnp.bfloat16)
    return (packing, unpacking)


def regroup(row_block, select, block_rows):
    pieces = row_block.reshape(-1, block_rows, row_block.shape[-1])
    return jnp.einsum("sb,brf->srf", select, pieces)


def dither(grads, partial_value, bits_now):
    tok_rows = grads.shape[0]
    jitter = (bits_now.astype(jnp.float32) * 2.0 ** (-30) - 0.5).reshape(tok_rows, 2, KV_HEADS, 1)
    summed = (grads.astype(jnp.float32) + partial_value).reshape(tok_rows, 2, KV_HEADS, HEAD_DIM)
    rounded = summed + jitter * jnp.abs(summed) * 2.0 ** (-4)
    return rounded.reshape(tok_rows, 2, KV_HEADS * HEAD_DIM).astype(jnp.bfloat16)


def local(
    queries, key_vectors, activations, value_weight, attended_grad, doc_ids, shard_plan, round_bits
):
    cycle_size = lax.axis_size("ctx")
    device_index = lax.axis_index("ctx")
    tok_rows = queries.shape[1]
    kv_width = key_vectors.shape[2]
    group_size = HEADS // KV_HEADS
    block_rows = tok_rows // BPD
    capacity = max(1, BPD // cycle_size)
    whole_rows = tok_rows * cycle_size
    scale_factor = HEAD_DIM ** (-0.5)
    plan_row = shard_plan[0]
    doc_row = doc_ids[0]
    places = jnp.arange(whole_rows, dtype=jnp.int32)
    place_pos = jnp.take(plan_row, places // block_rows) * block_rows + places % block_rows
    place_doc = jnp.take(doc_row, place_pos)
    packing, unpacking = block_maps(plan_row, device_index, cycle_size, BPD, capacity)
    query_rows = queries[0]
    key_rows = key_vectors[0]
    act_rows = activations[0]
    grad_rows = attended_grad[0]

    def outbound(row_block):
        return regroup(row_block, packing, block_rows)

    def inbound(received):
        flat = received.reshape(-1, received.shape[-1])
        return regroup(flat, unpacking, block_rows).reshape(tok_rows, received.shape[-1])

    def homebound(row_block):
        return regroup(row_block, unpacking.T, block_rows)

    def arrived(received):
        flat = received.reshape(-1, received.shape[-1])
        return regroup(flat, packing.T, block_rows).reshape(tok_rows, received.shape[-1])

    arrived_rows = (
        lax.all_to_all(outbound(query_rows), "ctx", split_axis=0, concat_axis=0, tiled=True),
        lax.all_to_all(outbound(key_rows), "ctx", split_axis=0, concat_axis=0, tiled=True),
        lax.all_to_all(outbound(act_rows), "ctx", split_axis=0, concat_axis=0, tiled=True),
        lax.all_to_all(outbound(grad_rows), "ctx", split_axis=0, concat_axis=0, tiled=True),
    )
    query_bal, key_bal, act_bal, grad_bal = [inbound(received) for received in arrived_rows]
    columns = act_bal
    value_bal = jnp.dot(
        columns,
        lax.all_gather(value_weight, ("dp", "ctx"), axis=0, tiled=True),
        preferred_element_type=jnp.float32,
    ).astype(jnp.bfloat16)
    my_pos = lax.dynamic_slice_in_dim(place_pos, device_index * tok_rows, tok_rows)
    my_doc = lax.dynamic_slice_in_dim(place_doc, device_index * tok_rows, tok_rows)
    query_lead = query_bal.reshape(tok_rows, KV_HEADS, group_size, HEAD_DIM).transpose(1, 2, 0, 3)
    grad_lead = grad_bal.reshape(tok_rows, KV_HEADS, group_size, HEAD_DIM).transpose(1, 2, 0, 3)

    def owner_slice(source_array, owner_index):
        return lax.dynamic_slice_in_dim(source_array, owner_index * tok_rows, tok_rows, 0)

    def head_lead(row_part):
        return row_part.reshape(-1, KV_HEADS, HEAD_DIM).transpose(1, 0, 2)

    def tile_mask(key_pos, key_doc):
        return (my_doc[:, None] == key_doc[None, :]) & (key_pos[None, :] <= my_pos[:, None])

    online_state = (
        jnp.full((KV_HEADS, group_size, tok_rows), -jnp.inf, jnp.float32),
        jnp.zeros((KV_HEADS, group_size, tok_rows), jnp.float32),
        jnp.zeros((KV_HEADS, group_size, tok_rows, HEAD_DIM), jnp.float32),
    )
    key_now, value_now = (key_bal, value_bal)
    for turn_index in range(cycle_size):
        owner_index = (device_index - turn_index) % cycle_size
        key_part, value_part = (key_now, value_now)
        absorb_running_top, absorb_running_sum, absorb_running_out = online_state
        absorb_key_heads = head_lead(key_part)
        absorb_value_heads = head_lead(value_part)
        absorb_allowed = tile_mask(
            owner_slice(place_pos, owner_index), owner_slice(place_doc, owner_index)
        )
        absorb_scores = jnp.einsum(
            "kgtd,knd->kgtn", query_lead, absorb_key_heads, preferred_element_type=jnp.float32
        )
        masked = jnp.where(absorb_allowed, absorb_scores * scale_factor, -jnp.inf)
        new_top = jnp.maximum(absorb_running_top, jnp.max(masked, axis=-1))
        weights = jnp.exp(masked - new_top[..., None])
        factor = jnp.exp(absorb_running_top - new_top)
        absorb_running_sum = absorb_running_sum * factor + jnp.sum(weights, axis=-1)
        update = jnp.einsum(
            "kgtn,knd->kgtd",
            weights.astype(jnp.bfloat16),
            absorb_value_heads,
            preferred_element_type=jnp.float32,
        )
        absorb_running_out = absorb_running_out * factor[..., None] + update
        online_state = (new_top, absorb_running_sum, absorb_running_out)
        if turn_index + 1 < cycle_size:
            key_now, value_now = shifted((key_now, value_now), "ctx", 1)
    running_top, running_sum, running_out = online_state
    attended_heads = (running_out / running_sum[..., None]).astype(jnp.bfloat16)
    log_total = running_top + jnp.log(running_sum)
    row_delta = jnp.sum(grad_lead.astype(jnp.float32) * attended_heads.astype(jnp.float32), axis=-1)
    attended_bal = attended_heads.transpose(2, 0, 1, 3).reshape(tok_rows, HEADS * HEAD_DIM)
    grads = jnp.zeros((tok_rows, 2, kv_width), jnp.bfloat16)
    query_acc = jnp.zeros((KV_HEADS, group_size, tok_rows, HEAD_DIM), jnp.float32)
    key_now, value_now = (key_bal, value_bal)
    for turn_index in range(cycle_size):
        owner_index = (device_index - turn_index) % cycle_size
        key_part, value_part = (key_now, value_now)
        key_heads = head_lead(key_part)
        value_heads = head_lead(value_part)
        allowed = tile_mask(
            owner_slice(place_pos, owner_index), owner_slice(place_doc, owner_index)
        )
        scores = jnp.einsum(
            "kgtd,knd->kgtn", query_lead, key_heads, preferred_element_type=jnp.float32
        )
        probability = jnp.where(allowed, jnp.exp(scores * scale_factor - log_total[..., None]), 0.0)
        prob_grad = jnp.einsum(
            "kgtd,knd->kgtn", grad_lead, value_heads, preferred_element_type=jnp.float32
        )
        score_grad = (probability * (prob_grad - row_delta[..., None])).astype(jnp.bfloat16)
        prob_low = probability.astype(jnp.bfloat16)
        query_acc = query_acc + jnp.einsum(
            "kgtn,knd->kgtd", score_grad, key_heads, preferred_element_type=jnp.float32
        )
        key_term = (
            jnp.einsum("kgtn,kgtd->nkd", score_grad, query_lead, preferred_element_type=jnp.float32)
            * scale_factor
        )
        value_term = jnp.einsum(
            "kgtn,kgtd->nkd", prob_low, grad_lead, preferred_element_type=jnp.float32
        )
        partial_value = jnp.stack(
            [key_term.reshape(tok_rows, kv_width), value_term.reshape(tok_rows, kv_width)], axis=1
        )
        bits_now = lax.dynamic_slice_in_dim(
            round_bits[turn_index], owner_index * tok_rows, tok_rows, 0
        )
        grads = dither(grads, partial_value, bits_now)
        if turn_index + 1 < cycle_size:
            key_now, value_now, grads = shifted((key_now, value_now, grads), "ctx", 1)
    grads = shifted(grads, "ctx", 1)
    key_grad_bal = grads[:, 0]
    value_grad_bal = grads[:, 1]
    query_grad_bal = (
        (query_acc * scale_factor)
        .astype(jnp.bfloat16)
        .transpose(2, 0, 1, 3)
        .reshape(tok_rows, HEADS * HEAD_DIM)
    )
    returned = (
        lax.all_to_all(homebound(attended_bal), "ctx", split_axis=0, concat_axis=0, tiled=True),
        lax.all_to_all(homebound(query_grad_bal), "ctx", split_axis=0, concat_axis=0, tiled=True),
        lax.all_to_all(homebound(key_grad_bal), "ctx", split_axis=0, concat_axis=0, tiled=True),
    )
    attended_out, query_out, key_out = [arrived(received) for received in returned]
    columns = act_bal
    weight_grad = lax.psum_scatter(
        lax.dot_general(
            columns, value_grad_bal, (((0,), (0,)), ((), ())), preferred_element_type=jnp.float32
        ),
        ("dp", "ctx"),
        scatter_dimension=0,
        tiled=True,
    )
    return (attended_out[None], query_out[None], key_out[None], weight_grad)


def solution(mesh):
    in_specs = (
        P("dp", "ctx", None),
        P("dp", "ctx", None),
        P("dp", "ctx", None),
        P(("dp", "ctx"), None),
        P("dp", "ctx", None),
        P("dp", None),
        P("dp", None),
        P(),
    )
    out_specs = (
        P("dp", "ctx", None),
        P("dp", "ctx", None),
        P("dp", "ctx", None),
        P(("dp", "ctx"), None),
    )
    return jax.shard_map(local, mesh=mesh, in_specs=in_specs, out_specs=out_specs, check_vma=False)
```

profile of v0, /device:TPU:136, one launch (start us, length us, event | category | flops | bytes accessed | tf_op | source)
XLA Modules:
  0.0 2301.8 jit_solution(9265732113816292888)
XLA Ops:
  10.4 6.0 all-to-all-start.1
  28.5 4.3 compare_select_fusion.2
  32.8 15.6 select_select_fusion
  51.6 7.2 all-to-all-start
  61.3 4.5 gather_fusion.1
  65.9 23.8 %collective-permute-done = bf16[128,512]{1,0:T(8,128)(2,1)S(1)} collective-permute-done((bf16[128,512]{1,0:T(8,128)(2,1)S(1)}, bf16[128,512]{1,0:T(8,128)(2,1)S(1)}, u32[]{:S(2)}, u32[]{:S(2)}) %collective-permute-start) | collective-permute-done | bytes 131104 | tf_op jit(solution)/shard_map/ppermute | solution.py:14
  89.7 8.6 collective-permute-done.2
  98.3 8.6 collective-permute-done.4
  107.7 7.9 collective-permute-done.6
  116.8 7.4 collective-permute-done.8
  125.1 4.3 copy.451
  154.5 7.3 all-to-all-start.4
  161.9 3.1 fusion.17
  180.6 5.4 all-to-all-done.4
  186.0 4.4 all-to-all-start.2
  190.5 4.1 fusion.11
  204.2 14.1 all-to-all-done.2
  218.2 4.1 fusion.15
  224.6 3.2 fusion.64
  234.0 3.3 fusion.60
  243.3 3.3 fusion.56
  257.5 465.9 %all-gather.2.cloned.1.call-done = bf16[4096,512]{1,0:T(8,128)(2,1)} async-done(((bf16[16,512]{1,0:T(8,128)(2,1)}), bf16[4096,512]{1,0:T(8,128)(2,1)}) %all-gather.2.cloned.1.call-update) | async-done | bytes 4194320 | tf_op jit(solution)/shard_map/all_gather | solution.py:102
  723.3 3.6 convolution_convert_fusion
  728.5 17.2 collective-permute-start.1
  751.5 3.4 collective-permute-start.3
  755.0 3.6 fusion.80
  762.8 3.6 fusion.78
  766.4 5.3 collective-permute-done.5
  773.3 3.6 fusion.76
  776.9 5.3 collective-permute-done.7
  783.9 3.7 fusion.74
  787.5 5.2 collective-permute-done.9
  794.4 3.7 fusion.72
  798.1 5.2 collective-permute-done.11
  805.4 3.6 fusion.70
  809.0 5.3 collective-permute-done.13
  816.1 8.8 fusion.1
  826.4 4.4 multiply_reduce_fusion
  830.9 2.8 multiply_convert_fusion.8
  843.5 2.7 fusion.51
  851.9 2.7 fusion.50
  856.3 2.8 fusion.49
  874.1 3.0 multiply_convert_fusion.3
  877.1 2.8 copy.530
  879.9 3.6 collective-permute-done.15
  896.7 3.0 collective-permute-start.17
  899.7 3.0 multiply_convert_fusion.2
  902.7 2.8 copy.536
  905.5 3.9 collective-permute-done.17
  916.5 6.3 collective-permute-done.18
  925.1 3.0 multiply_convert_fusion.1
  928.1 2.8 copy.542
  930.9 5.1 collective-permute-done.19
  938.8 8.3 collective-permute-done.20
  947.3 10.0 collective-permute-done.21
  957.3 4.6 fusion.179
  978.4 11.1 all-to-all-start.5
  996.6 24.5 %all-to-all-done.5 = bf16[8,32,4096]{2,1,0:T(8,128)(2,1)S(1)} async-done(((bf16[8,32,4096]{2,1,0:T(8,128)(2,1)}), bf16[8,32,4096]{2,1,0:T(8,128)(2,1)S(1)}, u32[]{:S(2)}, u32[]{:S(2)}) %all-to-all-start.5) | async-done | bytes 2097184 | tf_op jit(solution)/shard_map/all_to_all | solution.py:207
  1022.5 3.6 all-to-all-start.3
  1026.1 4.1 fusion.9
  1032.9 13.5 all-to-all-done.3
  1046.4 3.4 all-to-all-start.6
  1053.8 4.9 all-to-all-done.6
  1059.7 1234.8 %reduce-scatter.2.cloned.1.call-done = f32[16,512]{1,0:T(8,128)} async-done(((f32[4096,512]{1,0:T(8,128)}), f32[16,512]{1,0:T(8,128)}) %reduce-scatter.2.cloned.1.call-update) | async-done | bytes 32784 | tf_op jit(solution)/shard_map/reduce_scatter | solution.py:212
  (564 shorter events, 210.3 us)
Async XLA Ops:
  7.2 15.0 copy-start
  8.3 17.7 copy-start.164
  9.6 14.0 copy-start.48
  10.4 41.2 %all-to-all-start.1 = ((bf16[8,32,512]{2,1,0:T(8,128)(2,1)}), bf16[8,32,512]{2,1,0:T(8,128)(2,1)S(1)}, u32[]{:S(2)}, u32[]{:S(2)}) async-start(bf16[8,32,512]{2,1,0:T(8,128)(2,1)} %copy.397), calls=%async_computation.1 | async-start | bytes 524288 | tf_op jit(solution)/shard_map/all_to_all | solution.py:94
  16.4 706.9 %all-gather.2.cloned.1.call-start = ((), (), s32[]{:S(2)}) async-start(), calls=%async_computation.8 | async-start | bytes 4210688 | tf_op jit(solution)/shard_map/all_gather | solution.py:102
  51.6 103.0 %all-to-all-start = ((bf16[8,32,4096]{2,1,0:T(8,128)(2,1)}), bf16[8,32,4096]{2,1,0:T(8,128)(2,1)S(1)}, u32[]{:S(2)}, u32[]{:S(2)}) async-start(bf16[8,32,4096]{2,1,0:T(8,128)(2,1)} %copy.393), calls=%async_computation | async-start | bytes 4194304 | tf_op jit(solution)/shard_map/all_to_all | solution.py:93
  59.2 30.4 %collective-permute-start = (bf16[128,512]{1,0:T(8,128)(2,1)S(1)}, bf16[128,512]{1,0:T(8,128)(2,1)S(1)}, u32[]{:S(2)}, u32[]{:S(2)}) collective-permute-start(bf16[128,512]{1,0:T(8,128)(2,1)S(1)} %bitcast.689), channel_id=1, source_target_pairs={{0,1},{1,2},{2,3},{3,4},{4,5},{5,6},{6,7},{7,0},{8,9},{9,10},{10,1... | collective-permute-start | bytes 393224 | tf_op jit(solution)/shard_map/ppermute | solution.py:14
  61.3 28.3 %copy-start.95 = (s32[8,1024,8]{1,2,0:T(8,128)S(1)}, s32[8,1024,8]{1,2,0:T(8,128)}, u32[]{:S(2)}) copy-start(s32[8,1024,8]{1,2,0:T(8,128)} %param.15) | copy-start | bytes 786436
  89.6 8.7 collective-permute-start.2
  98.3 8.6 collective-permute-start.4
  107.0 8.6 collective-permute-start.6
  115.6 8.7 collective-permute-start.8
  124.2 21.1 collective-permute-start.10
  145.3 8.9 collective-permute-start.12
  147.1 20.8 copy-start.97
  147.1 30.4 %copy-start.68 = (bf16[128,4,128]{2,1,0:T(4,128)(2,1)}, bf16[128,4,128]{2,1,0:T(4,128)(2,1)S(1)}, u32[]{:S(2)}) copy-start(bf16[128,4,128]{2,1,0:T(4,128)(2,1)S(1)} %reshape_reshape.17) | copy-start | bytes 393220
  148.3 27.6 %copy-start.70 = (bf16[128,4,128]{2,0,1:T(8,128)(2,1)}, bf16[128,4,128]{2,0,1:T(8,128)(2,1)S(1)}, u32[]{:S(2)}) copy-start(bf16[128,4,128]{2,0,1:T(8,128)(2,1)S(1)} %copy.416) | copy-start | bytes 393220
  154.5 31.5 %all-to-all-start.4 = ((bf16[8,32,4096]{2,1,0:T(8,128)(2,1)}), bf16[8,32,4096]{2,1,0:T(8,128)(2,1)}, u32[]{:S(2)}, u32[]{:S(2)}) async-start(bf16[8,32,4096]{2,1,0:T(8,128)(2,1)} %copy.451), calls=%async_computation.4 | async-start | bytes 4194304 | tf_op jit(solution)/shard_map/all_to_all | solution.py:96
  165.8 11.7 copy-start.50
  167.9 10.4 copy-start.141
  176.6 18.0 copy-start.19
  178.4 24.2 %copy-start.86 = (f32[4,8,128]{2,1,0:T(8,128)}, f32[4,8,128]{2,1,0:T(8,128)S(1)}, u32[]{:S(2)}) copy-start(f32[4,8,128]{2,1,0:T(8,128)S(1)} %get-tuple-element.24) | copy-start | bytes 49156
  178.4 24.2 %copy-start.88 = (f32[4,8,128]{2,1,0:T(8,128)}, f32[4,8,128]{2,1,0:T(8,128)S(1)}, u32[]{:S(2)}) copy-start(f32[4,8,128]{2,1,0:T(8,128)S(1)} %get-tuple-element.25) | copy-start | bytes 49156
  178.4 24.2 %copy-start.89 = (f32[4,8,128]{2,1,0:T(8,128)}, f32[4,8,128]{2,1,0:T(8,128)S(1)}, u32[]{:S(2)}) copy-start(f32[4,8,128]{2,1,0:T(8,128)S(1)} %get-tuple-element.26) | copy-start | bytes 49156
  178.4 24.2 %copy-start.91 = (f32[4,8,128]{2,1,0:T(8,128)}, f32[4,8,128]{2,1,0:T(8,128)S(1)}, u32[]{:S(2)}) copy-start(f32[4,8,128]{2,1,0:T(8,128)S(1)} %get-tuple-element.27) | copy-start | bytes 49156
  178.4 24.2 %copy-start.92 = (f32[4,8,128]{2,1,0:T(8,128)}, f32[4,8,128]{2,1,0:T(8,128)S(1)}, u32[]{:S(2)}) copy-start(f32[4,8,128]{2,1,0:T(8,128)S(1)} %get-tuple-element.28) | copy-start | bytes 49156
  178.4 24.2 %copy-start.94 = (f32[4,8,128]{2,1,0:T(8,128)}, f32[4,8,128]{2,1,0:T(8,128)S(1)}, u32[]{:S(2)}) copy-start(f32[4,8,128]{2,1,0:T(8,128)S(1)} %get-tuple-element.29) | copy-start | bytes 49156
  178.4 24.2 %copy-start.96 = (f32[4,8,128]{2,1,0:T(8,128)}, f32[4,8,128]{2,1,0:T(8,128)S(1)}, u32[]{:S(2)}) copy-start(f32[4,8,128]{2,1,0:T(8,128)S(1)} %get-tuple-element.23) | copy-start | bytes 49156
  180.1 22.6 copy-start.116
  180.6 22.1 copy-start.118
  186.0 32.2 %all-to-all-start.2 = ((bf16[8,32,4096]{2,1,0:T(8,128)(2,1)}), bf16[8,32,4096]{2,1,0:T(8,128)(2,1)}, u32[]{:S(2)}, u32[]{:S(2)}) async-start(bf16[8,32,4096]{2,1,0:T(8,128)(2,1)} %copy.403), calls=%async_computation.2 | async-start | bytes 4194304 | tf_op jit(solution)/shard_map/all_to_all | solution.py:95
  190.4 2104.1 %reduce-scatter.2.cloned.1.call-start = ((), (), s32[]{:S(2)}) async-start(), calls=%async_computation.9 | async-start | bytes 8421376 | tf_op jit(solution)/shard_map/reduce_scatter | solution.py:212
  203.4 14.8 copy-start.162
  728.5 21.3 collective-permute-start.1
  751.5 9.6 collective-permute-start.3
  762.8 8.9 collective-permute-start.5
  773.3 8.9 collective-permute-start.7
  773.3 10.6 copy-start.90
  783.9 8.9 collective-permute-start.9
  794.4 8.9 collective-permute-start.11
  794.4 11.0 copy-start.87
  805.0 9.3 collective-permute-start.13
  816.0 10.3 copy-start.40
  816.0 10.3 copy-start.151
  837.7 17.0 copy-start.32
  850.0 21.1 collective-permute-start.14
  873.2 10.3 collective-permute-start.15
  884.4 10.3 collective-permute-start.16
  888.4 11.2 copy-start.12
  888.4 11.2 copy-start.99
  896.7 12.7 collective-permute-start.17
  910.3 12.6 copy-start.59
  910.3 12.5 collective-permute-start.18
  912.8 12.3 copy-start.28
  912.8 12.3 copy-start.138
  924.9 11.1 collective-permute-start.19
  936.9 10.2 collective-permute-start.20
  947.2 10.1 collective-permute-start.21
  978.4 11.1 copy-start.29
  978.4 42.7 %all-to-all-start.5 = ((bf16[8,32,4096]{2,1,0:T(8,128)(2,1)}), bf16[8,32,4096]{2,1,0:T(8,128)(2,1)S(1)}, u32[]{:S(2)}, u32[]{:S(2)}) async-start(bf16[8,32,4096]{2,1,0:T(8,128)(2,1)} %copy.497), calls=%async_computation.5 | async-start | bytes 4194304 | tf_op jit(solution)/shard_map/all_to_all | solution.py:207
  996.6 29.5 %copy-start.165 = (s32[4]{0:T(128)S(1)}, s32[4]{0:T(128)}, u32[]{:S(2)}) copy-start(s32[4]{0:T(128)} %copy-done.164) | copy-start | bytes 52
  1022.5 23.9 %all-to-all-start.3 = ((bf16[8,32,4096]{2,1,0:T(8,128)(2,1)}), bf16[8,32,4096]{2,1,0:T(8,128)(2,1)S(1)}, u32[]{:S(2)}, u32[]{:S(2)}) async-start(bf16[8,32,4096]{2,1,0:T(8,128)(2,1)} %copy.447), calls=%async_computation.3 | async-start | bytes 4194304 | tf_op jit(solution)/shard_map/all_to_all | solution.py:206
  1046.4 12.4 all-to-all-start.6
  1049.8 1244.7 %copy-start.1 = (bf16[1,128,4096]{2,1,0:T(8,128)(2,1)S(1)}, bf16[1,128,4096]{2,1,0:T(8,128)(2,1)}, u32[]{:S(2)}) copy-start(bf16[1,128,4096]{2,1,0:T(8,128)(2,1)} %param.8) | copy-start | bytes 3145732
  (140 other events, 609.2 us)
Sparse Core Ops, SparseCore 0:
  19.1 704.1 all-gather.1
  962.1 1332.3 reduce-scatter.1
where the time goes:
time: 2310 us; the launch traced here: 2300 us
  waiting for transfers between devices  1890 us (82%)
  matrix products  145 us (6%)
  local copies, waits for them, and re-layouts  127 us (5%)
  starting transfers between devices  72.5 us (3%)
  other arithmetic  48.5 us (2%)
    reduce_scatter x1, waiting for transfers between devices, local(): lax.psum_scatter(lax.dot_general(columns, value_grad_bal, (((0,), (0,)),...  1230 us
    all_gather x1, waiting for transfers between devices, local(): lax.all_gather(value_weight, ('dp', 'ctx'), axis=0, tiled=True)  466 us
    ppermute x22, waiting for transfers between devices, shifted(): lax.ppermute(x, axis, [(i, (i + by) % devices) for i in range(devices)])  128 us
  transfers between devices with their start and end apart: 31, of which 27 were waited for; matrix products, arithmetic and copies ran while one was open for 11% of the time, Pallas kernels for 0%

commit v1 on v0

v1 whole, which is shorter than its diff:
```python
import functools

import jax
import jax.numpy as jnp
from jax import lax
from jax.experimental import pallas as pl
from jax.experimental.pallas import tpu as pltpu
from jax.sharding import PartitionSpec as P

MESH = pl.DeviceIdType.MESH
ANY = pl.BlockSpec(memory_space=pl.ANY)
BF = jnp.bfloat16
F32 = jnp.float32
I32 = jnp.int32

N_CTX = 8
N_Z = 8
HEAD = 128
GROUP = 8
TOK = 128
HALF = 64
SEQ = 1024
BLOCK = 32
BAND = 512
WIN = BAND + BLOCK
D = 4096
KVW = 512
COLS = 256
PAD_ROWS = SEQ + BAND + 128
SCALE = HEAD**-0.5
LOG2E = 1.4426950408889634
NEG = -1e30


def vmem(shape, dtype):
    return pltpu.VMEM(shape, dtype)


def dma(*shape):
    return pltpu.SemaphoreType.DMA(shape)


class Place:
    def __init__(self):
        self.dp = lax.axis_index("dp")
        self.ctx = lax.axis_index("ctx")
        self.core = self.dp % 2
        self.z = (self.dp // 2) % N_Z
        self.ylo = self.dp // 16
        self.base = self.dp - self.core
        self.par = self.ctx // 4
        self.head = self.ctx % 4
        self.partner = (self.base + 1 - self.core, self.ctx)
        self.across = (self.dp + 16 - 32 * self.ylo, self.ctx)
        self.up = (self.ylo * 16 + (self.z + 1) % N_Z * 2 + self.core, self.ctx)
        self.down = (self.ylo * 16 + (self.z + N_Z - 1) % N_Z * 2 + self.core, self.ctx)

    def is_me(self, core, ctx):
        return (self.core == core) & (self.ctx == ctx)


def greet(me):
    barrier = pltpu.get_barrier_semaphore()
    for core in range(2):
        for ctx in range(N_CTX):

            @pl.when(jnp.logical_not(me.is_me(core, ctx)))
            def _(core=core, ctx=ctx):
                pl.semaphore_signal(barrier, inc=1, device_id=(me.base + core, jnp.int32(ctx)), device_id_type=MESH)

    for other in (me.across, me.up, me.down):
        pl.semaphore_signal(barrier, inc=1, device_id=other, device_id_type=MESH)
    pl.semaphore_wait(barrier, 2 * N_CTX + 2)


def remote(src, dst, ssem, rsem, device):
    return pltpu.make_async_remote_copy(
        src_ref=src, dst_ref=dst, send_sem=ssem, recv_sem=rsem, device_id=device, device_id_type=MESH
    )


def push(me, src, dst, ssem, rsem, core, ctx):
    mine = me.is_me(core, ctx)

    @pl.when(mine)
    def _():
        pltpu.make_async_copy(src, dst, rsem).start()

    @pl.when(jnp.logical_not(mine))
    def _():
        remote(src, dst, ssem, rsem, (me.base + core, jnp.int32(ctx))).start()


def pushed(me, src, ssem, core, ctx):
    @pl.when(jnp.logical_not(me.is_me(core, ctx)))
    def _():
        remote(src, src, ssem, ssem, (me.base + core, jnp.int32(ctx))).wait_send()


def landed(dst, rsem):
    pltpu.make_async_copy(dst, dst, rsem).wait()


def in_kernel(
    q, g, k, x, w, lens, plc, qa, ga, ka, va, lensp, plcp,
    wfull, xv, vbuf, vacc,
    w_s, w_r, q_s, q_r, g_s, g_r, k_s, k_r, v_s, v_r, one_s, one_r, up_s, up_r, dn_s, dn_r, loc,
):
    me = Place()
    greet(me)
    plane = [(core, ctx) for core in range(2) for ctx in range(N_CTX)]

    def w_src(core):
        return w.at[:, pl.ds(core * COLS, COLS)]

    row = pl.multiple_of(me.core * 128 + me.ctx * 16, 16)
    w_dst = wfull.at[me.ylo, me.z, pl.ds(row, 16), :]
    for n, (core, ctx) in enumerate(plane):
        push(me, w_src(core), w_dst, w_s.at[n], w_r.at[me.core * N_CTX + me.ctx], core, ctx)

    own_x = pltpu.make_async_copy(x, xv.at[me.core], loc.at[0])
    own_l = pltpu.make_async_copy(lens, lensp.at[me.core], loc.at[1])
    own_p = pltpu.make_async_copy(plc, plcp.at[me.core], loc.at[2])
    far_x = remote(x, xv.at[me.core], one_s.at[0], one_r.at[0], me.partner)
    far_l = remote(lens, lensp.at[me.core], one_s.at[1], one_r.at[1], me.partner)
    far_p = remote(plc, plcp.at[me.core], one_s.at[2], one_r.at[2], me.partner)
    for copy in (own_x, far_x, own_l, far_l, own_p, far_p):
        copy.start()

    def k_src(j):
        return k.at[:, pl.ds(j * HEAD, HEAD)]

    def wide(ref, core, j):
        return ref.at[pl.ds(core * HALF, HALF), pl.ds(j * GROUP * HEAD, GROUP * HEAD)]

    spot = pl.multiple_of(me.ctx * TOK, TOK)
    half_spot = pl.multiple_of(me.ctx * HALF, HALF)

    for n in range(8):
        core, j = n // 4, n % 4
        push(me, k_src(j), ka.at[pl.ds(spot, TOK), :], k_s.at[n], k_r.at[me.ctx], core, me.core * 4 + j)
    for n in range(8):
        core, j = n // 4, n % 4
        push(me, wide(q, core, j), qa.at[pl.ds(half_spot, HALF), :], q_s.at[n], q_r.at[me.ctx], core, me.core * 4 + j)
    for n in range(8):
        core, j = n // 4, n % 4
        push(me, wide(g, core, j), ga.at[pl.ds(half_spot, HALF), :], g_s.at[n], g_r.at[me.ctx], core, me.core * 4 + j)

    for n in range(16):
        landed(wfull.at[me.ylo, me.z, pl.ds(n * 16, 16), :], w_r.at[n])
    mine = wfull.at[me.ylo, me.z]
    over = remote(mine, mine, one_s.at[3], one_r.at[3], me.across)
    over.start()
    own_x.wait()
    far_x.wait()
    vacc[...] = jnp.zeros_like(vacc)
    over.wait()

    def project(z):
        for ylo in range(2):
            col = pl.multiple_of(ylo * 2048 + z * 256, 256)
            part = xv[:, :, pl.ds(col, 256)].reshape(2 * TOK, 256)
            vacc[...] += jnp.dot(part, wfull[ylo, z], preferred_element_type=F32)

    def chunk(z):
        return wfull.at[:, z]

    for s in range(4):
        z_up = (me.z + N_Z - s) % N_Z
        up = remote(chunk(z_up), chunk(z_up), up_s.at[s], up_r.at[s], me.up)
        up.start()
        if s < 3:
            z_dn = (me.z + s) % N_Z
            dn = remote(chunk(z_dn), chunk(z_dn), dn_s.at[s], dn_r.at[s], me.down)
            dn.start()
        project(z_up)
        if s > 0:
            project((me.z + s) % N_Z)
        up.wait()
        if s < 3:
            dn.wait()
    project((me.z + N_Z - 4) % N_Z)

    vbuf[...] = vacc[...].astype(BF)

    def v_src(par, jj):
        return vbuf.at[pl.ds(par * TOK, TOK), pl.ds(jj * HEAD, HEAD)]

    routes = [(core, par, jj) for core in range(2) for par in range(2) for jj in range(2)]
    for n, (core, par, jj) in enumerate(routes):
        push(
            me, v_src(par, jj), va.at[pl.ds(spot, TOK), :], v_s.at[n], v_r.at[me.ctx], core,
            par * 4 + me.core * 2 + jj,
        )

    for n, (core, ctx) in enumerate(plane):
        pushed(me, w_src(core), w_s.at[n], core, ctx)
    for n in range(8):
        core, j = n // 4, n % 4
        pushed(me, k_src(j), k_s.at[n], core, me.core * 4 + j)
        pushed(me, wide(q, core, j), q_s.at[n], core, me.core * 4 + j)
        pushed(me, wide(g, core, j), g_s.at[n], core, me.core * 4 + j)
    for n, (core, par, jj) in enumerate(routes):
        pushed(me, v_src(par, jj), v_s.at[n], core, par * 4 + me.core * 2 + jj)
    for copy in (own_l, far_l, own_p, far_p):
        copy.wait()
    for i in range(N_CTX):
        landed(ka.at[pl.ds(i * TOK, TOK), :], k_r.at[i])
        landed(qa.at[pl.ds(i * HALF, HALF), :], q_r.at[i])
        landed(ga.at[pl.ds(i * HALF, HALF), :], g_r.at[i])
        landed(va.at[pl.ds(i * TOK, TOK), :], v_r.at[i])


def exchange_in(q, g, k, x, w, lens, plc):
    return pl.pallas_call(
        in_kernel,
        out_shape=[
            jax.ShapeDtypeStruct((SEQ // 2, GROUP * HEAD), BF),
            jax.ShapeDtypeStruct((SEQ // 2, GROUP * HEAD), BF),
            jax.ShapeDtypeStruct((SEQ, HEAD), BF),
            jax.ShapeDtypeStruct((SEQ, HEAD), BF),
            jax.ShapeDtypeStruct((2,) + lens.shape, I32),
            jax.ShapeDtypeStruct((2,) + plc.shape, I32),
        ],
        in_specs=[ANY] * 7,
        out_specs=[ANY] * 6,
        scratch_shapes=[
            vmem((2, N_Z, 256, COLS), BF), vmem((2, TOK, D), BF), vmem((2 * TOK, COLS), BF), vmem((2 * TOK, COLS), F32),
            dma(16), dma(16), dma(8), dma(8), dma(8), dma(8), dma(8), dma(8), dma(8), dma(8),
            dma(4), dma(4), dma(4), dma(4), dma(3), dma(3), dma(3),
        ],
        compiler_params=pltpu.CompilerParams(
            collective_id=0, has_side_effects=True, vmem_limit_bytes=24 * 2**20
        ),
        cost_estimate=pl.CostEstimate(flops=2 * 256 * D * COLS, bytes_accessed=16 * 2**20, transcendentals=0),
        name="exchange_in",
    )(q, g, k, x, w, lens, plc)


NT = (((1,), (1,)), ((), ()))
TN = (((0,), (0,)), ((), ()))


def attention_kernel(
    plc, q, g, k, v, lens, bits, o, dq, terms, dith,
    kpad, vpad, kt, vt, kacc, vacc,
):
    me = Place()
    step = pl.program_id(0)
    core, par = me.core, me.par

    @pl.when(step == 0)
    def _():
        for pad, src in ((kpad, k), (vpad, v)):
            pad[0:BAND, :] = jnp.zeros((BAND, HEAD), BF)
            pad[BAND : BAND + SEQ, :] = src[...]
            pad[BAND + SEQ :, :] = jnp.zeros((PAD_ROWS - BAND - SEQ, HEAD), BF)
        for b in range(2):
            off = core * HALF + b * BLOCK
            for n in range(12):
                rows = pl.ds(pl.multiple_of(off + n * 128, BLOCK), 128)
                kt[b, :, n * 128 : n * 128 + 128] = kpad[rows, :].T
                vt[b, :, n * 128 : n * 128 + 128] = vpad[rows, :].T

        @pl.loop(0, N_CTX)
        def _(c):
            kacc[c] = jnp.zeros((BAND + SEQ, HEAD), F32)
            vacc[c] = jnp.zeros((BAND + SEQ, HEAD), F32)

    key_row = lax.broadcasted_iota(I32, (WIN, GROUP * BLOCK), 0)
    lane = lax.broadcasted_iota(I32, (1, GROUP * BLOCK), 1) % BLOCK
    for b in range(2):
        block = step * 4 + core * 2 + b
        owner = plc[par, 0, block] // 4
        start = pl.multiple_of(block * BLOCK, BLOCK)
        rows = pl.ds(start, WIN)
        window = pl.ds(pl.multiple_of(step * TOK, TOK), WIN)

        def stacked(ref):
            return jnp.concatenate(
                [ref[b * BLOCK : (b + 1) * BLOCK, h * HEAD : (h + 1) * HEAD] for h in range(GROUP)], axis=0
            )

        def unstack(ref, value):
            for h in range(GROUP):
                ref[b * BLOCK : (b + 1) * BLOCK, h * HEAD : (h + 1) * HEAD] = value[h * BLOCK : (h + 1) * BLOCK]

        qs, gs = stacked(q), stacked(g)
        kw, vw = kpad[rows, :], vpad[rows, :]
        first = lane + BAND - lens[par, pl.ds(block, 1), :]
        allowed = (key_row >= first) & (key_row <= lane + BAND)
        s = lax.dot_general(kw, qs, NT, preferred_element_type=F32) * (SCALE * LOG2E)
        s = jnp.where(allowed, s, NEG)
        top = jnp.max(s, axis=0, keepdims=True)
        weight = jnp.exp2(s - top)
        prob = weight * (1.0 / jnp.sum(weight, axis=0, keepdims=True))
        low = prob.astype(BF)
        out_t = jnp.dot(vt[b, :, window], low, preferred_element_type=F32)
        out = out_t.T.astype(BF)
        unstack(o, out)
        gt = gs.astype(F32).T
        delta = jnp.sum(gt * out_t.astype(BF).astype(F32), axis=0, keepdims=True)
        dprob = lax.dot_general(vw, gs, NT, preferred_element_type=F32)
        dscore = (prob * (dprob - delta)).astype(BF)
        dq_t = jnp.dot(kt[b, :, window], dscore, preferred_element_type=F32)
        unstack(dq, (dq_t * SCALE).T.astype(BF))
        kacc[owner, rows, :] += jnp.dot(dscore, qs, preferred_element_type=F32)
        vacc[owner, rows, :] += jnp.dot(low, gs, preferred_element_type=F32)

    @pl.when(step == N_CTX - 1)
    def _():
        for half in range(2):

            @pl.loop(0, 16)
            def _(n):
                own = plc[par, 0, half * 16 + n] // 4
                src = pl.ds(pl.multiple_of(BAND + (half * 16 + n) * BLOCK, BLOCK), BLOCK)
                dst = pl.ds(pl.multiple_of(n * BLOCK, BLOCK), BLOCK)
                for t in range(N_CTX):
                    c = (own + t) % N_CTX
                    terms[half, 0, t, dst, :] = (kacc[c, src, :] * SCALE).astype(BF)
                    terms[half, 1, t, dst, :] = vacc[c, src, :].astype(BF)

        wanted = [bits[pl.ds(t * 8 + me.head, 1), :] for t in range(N_CTX)]
        wanted += [bits[pl.ds(t * 8 + 4 + me.head, 1), :] for t in range(N_CTX)]
        jitter = jnp.concatenate(wanted, axis=0).astype(F32) * 2.0**-30 - 0.5
        jitter = jnp.concatenate([jitter * 2.0**-4, jnp.zeros((112, SEQ), F32)], axis=0)
        kacc[0, 0:SEQ, :] = jitter.T

        @pl.loop(0, 16)
        def _(n):
            place = plc[par, 0, core * 16 + n]
            dst = pl.ds(pl.multiple_of(n * BLOCK, BLOCK), BLOCK)
            dith[dst, :] = kacc[0, pl.ds(pl.multiple_of(place * BLOCK, BLOCK), BLOCK), :]


def attend(plc, q, g, k, v, lens, bits):
    tile = pl.BlockSpec((HALF, GROUP * HEAD), lambda i, *_: (i, 0))

    def whole(shape):
        return pl.BlockSpec(shape, lambda i, *_: (0,) * len(shape))

    return pl.pallas_call(
        attention_kernel,
        grid_spec=pltpu.PrefetchScalarGridSpec(
            num_scalar_prefetch=1,
            grid=(N_CTX,),
            in_specs=[tile, tile, whole(k.shape), whole(v.shape), whole(lens.shape), whole(bits.shape)],
            out_specs=[tile, tile, whole((2, 2, N_CTX, SEQ // 2, HEAD)), whole((SEQ // 2, HEAD))],
            scratch_shapes=[
                vmem((PAD_ROWS, HEAD), BF), vmem((PAD_ROWS, HEAD), BF),
                vmem((2, HEAD, 1536), BF), vmem((2, HEAD, 1536), BF),
                vmem((N_CTX, BAND + SEQ, HEAD), F32), vmem((N_CTX, BAND + SEQ, HEAD), F32),
            ],
        ),
        out_shape=[
            jax.ShapeDtypeStruct((SEQ // 2, GROUP * HEAD), BF),
            jax.ShapeDtypeStruct((SEQ // 2, GROUP * HEAD), BF),
            jax.ShapeDtypeStruct((2, 2, N_CTX, SEQ // 2, HEAD), BF),
            jax.ShapeDtypeStruct((SEQ // 2, HEAD), F32),
        ],
        compiler_params=pltpu.CompilerParams(vmem_limit_bytes=50 * 2**20),
        cost_estimate=pl.CostEstimate(
            flops=12 * 16 * 256 * WIN * HEAD, bytes_accessed=12 * 2**20, transcendentals=16 * 256 * WIN
        ),
        name="attention",
    )(plc, q, g, k, v, lens, bits)


def out_kernel(
    oc, dqc, terms, dith, x, att, dqo, dko, wg,
    xv, own, part, dv_pair, kd, vd, jit, up_b, dn_b, up_in, dn_in, y_b, y_in, c_b, c_in, wsum,
    o_s, o_r, d_s, d_r, dk_s, dk_r, dv_s, dv_r, one_s, one_r, up_s, up_r, dn_s, dn_r, c_s, c_r, loc,
):
    me = Place()
    greet(me)
    away = 1 - me.core
    swap = remote(terms.at[away], part, one_s.at[0], one_r.at[0], me.partner)
    swap.start()
    keep = pltpu.make_async_copy(terms.at[me.core], own, loc.at[0])
    keep.start()
    jit_in = pltpu.make_async_copy(dith, jit, loc.at[1])
    jit_in.start()
    far_x = remote(x, xv.at[me.core], one_s.at[1], one_r.at[1], me.partner)
    far_x.start()
    own_x = pltpu.make_async_copy(x, xv.at[me.core], loc.at[2])
    own_x.start()

    def wide(ref, j):
        return ref.at[pl.ds(pl.multiple_of(me.core * HALF, HALF), HALF), pl.ds(pl.multiple_of(j * GROUP * HEAD, HEAD), GROUP * HEAD)]

    def home(ref, i):
        return ref.at[pl.ds(i * HALF, HALF), :]

    for src, dst, ssem, rsem in ((oc, att, o_s, o_r), (dqc, dqo, d_s, d_r)):
        for i in range(N_CTX):
            push(me, home(src, i), wide(dst, me.head), ssem.at[i], rsem.at[me.core * 4 + me.head], me.par, i)

    swap.wait()
    keep.wait()
    jit_in.wait()

    @pl.loop(0, 16)
    def _(n):
        rows = pl.ds(pl.multiple_of(n * BLOCK, BLOCK), BLOCK)
        noise = jit[rows, :]
        for f, out in ((0, kd), (1, vd)):
            acc = jnp.zeros((BLOCK, HEAD), F32)
            for t in range(N_CTX):
                total = acc + own[f, t, rows, :].astype(F32) + part[f, t, rows, :].astype(F32)
                u = noise[:, f * 8 + t : f * 8 + t + 1]
                acc = (total + u * jnp.abs(total)).astype(BF).astype(F32)
            out[rows, :] = acc.astype(BF)

    def tile(ref, n):
        return ref.at[pl.ds(n * TOK, TOK), :]

    v_core = me.head // 2
    v_col = pl.multiple_of(me.head % 2 * HEAD, HEAD)
    for n in range(4):
        push(
            me, tile(vd, n), dv_pair.at[pl.ds(pl.multiple_of(me.par * TOK, TOK), TOK), pl.ds(v_col, HEAD)],
            dv_s.at[n], dv_r.at[me.par * 2 + me.head % 2], v_core, me.core * 4 + n,
        )
    k_col = pl.multiple_of(me.head * HEAD, HEAD)
    for n in range(4):
        push(
            me, tile(kd, n), dko.at[:, pl.ds(k_col, HEAD)], dk_s.at[n], dk_r.at[me.head], me.par, me.core * 4 + n
        )
    own_x.wait()
    far_x.wait()
    for n in range(4):
        landed(dv_pair.at[pl.ds(n // 2 * TOK, TOK), pl.ds(n % 2 * HEAD, HEAD)], dv_r.at[n])

    def local_sum(z, ylo):
        col = pl.multiple_of(ylo * 2048 + z * 256, 256)
        return lax.dot_general(
            xv[:, :, pl.ds(col, 256)].reshape(2 * TOK, 256), dv_pair[...], TN, preferred_element_type=F32
        )

    for s in range(4):
        z_up = (me.z + 4 - s) % N_Z
        for ylo in range(2):
            total = local_sum(z_up, ylo)
            if s > 0:
                total = total + up_in[s - 1, ylo].astype(F32)
            up_b[s, ylo] = total.astype(BF)
        up = remote(up_b.at[s], up_in.at[s], up_s.at[s], up_r.at[s], me.up)
        up.start()
        if s < 3:
            z_dn = (me.z + N_Z - 3 + s) % N_Z
            for ylo in range(2):
                total = local_sum(z_dn, ylo)
                if s > 0:
                    total = total + dn_in[s - 1, ylo].astype(F32)
                dn_b[s, ylo] = total.astype(BF)
            dn = remote(dn_b.at[s], dn_in.at[s], dn_s.at[s], dn_r.at[s], me.down)
            dn.start()
        if s == 3:
            for ylo in range(2):
                wsum[ylo] = local_sum(me.z, ylo) + dn_in[2, ylo].astype(F32)
        up.wait()
        if s < 3:
            dn.wait()
    for ylo in range(2):
        wsum[ylo] += up_in[3, ylo].astype(F32)

    y_b[...] = wsum[1 - me.ylo].astype(BF)
    over = remote(y_b, y_in, one_s.at[2], one_r.at[2], me.across)
    over.start()
    over.wait()
    c_b[...] = (wsum[me.ylo] + y_in[...].astype(F32)).astype(BF)

    for n in range(16):
        push(
            me, c_b.at[pl.ds(n * 16, 16), :], c_in.at[me.core, me.ctx], c_s.at[n], c_r.at[me.core * N_CTX + me.ctx],
            n // N_CTX, n % N_CTX,
        )
    for n in range(16):
        landed(c_in.at[n // N_CTX, n % N_CTX], c_r.at[n])
    for core in range(2):
        total = c_in[core, 0].astype(F32)
        for i in range(1, N_CTX):
            total = total + c_in[core, i].astype(F32)
        wg[:, core * COLS : (core + 1) * COLS] = total

    for n in range(16):
        pushed(me, c_b.at[pl.ds(n * 16, 16), :], c_s.at[n], n // N_CTX, n % N_CTX)
    for n in range(4):
        pushed(me, tile(vd, n), dv_s.at[n], v_core, me.core * 4 + n)
        pushed(me, tile(kd, n), dk_s.at[n], me.par, me.core * 4 + n)
        landed(dko.at[:, pl.ds(n * HEAD, HEAD)], dk_r.at[n])
    for i in range(N_CTX):
        pushed(me, home(oc, i), o_s.at[i], me.par, i)
        pushed(me, home(dqc, i), d_s.at[i], me.par, i)
    for core in range(2):
        for j in range(4):
            dst = (pl.ds(core * HALF, HALF), pl.ds(j * GROUP * HEAD, GROUP * HEAD))
            landed(att.at[dst], o_r.at[core * 4 + j])
            landed(dqo.at[dst], d_r.at[core * 4 + j])


def exchange_out(oc, dqc, terms, dith, x):
    slab = (2, 256, COLS)
    return pl.pallas_call(
        out_kernel,
        out_shape=[
            jax.ShapeDtypeStruct((TOK, D), BF),
            jax.ShapeDtypeStruct((TOK, D), BF),
            jax.ShapeDtypeStruct((TOK, KVW), BF),
            jax.ShapeDtypeStruct((16, KVW), F32),
        ],
        in_specs=[ANY] * 5,
        out_specs=[ANY] * 3 + [pl.BlockSpec(memory_space=pltpu.VMEM)],
        scratch_shapes=[
            vmem((2, TOK, D), BF), vmem((2, N_CTX, SEQ // 2, HEAD), BF), vmem((2, N_CTX, SEQ // 2, HEAD), BF),
            vmem((2 * TOK, COLS), BF), vmem((SEQ // 2, HEAD), BF), vmem((SEQ // 2, HEAD), BF), vmem((SEQ // 2, HEAD), F32),
            vmem((4,) + slab, BF), vmem((3,) + slab, BF), vmem((4,) + slab, BF), vmem((3,) + slab, BF),
            vmem((256, COLS), BF), vmem((256, COLS), BF), vmem((256, COLS), BF), vmem((2, N_CTX, 16, COLS), BF),
            vmem(slab, F32),
            dma(8), dma(8), dma(8), dma(8), dma(4), dma(4), dma(4), dma(4), dma(3), dma(3),
            dma(4), dma(4), dma(3), dma(3), dma(16), dma(16), dma(3),
        ],
        compiler_params=pltpu.CompilerParams(
            collective_id=1, has_side_effects=True, vmem_limit_bytes=32 * 2**20
        ),
        cost_estimate=pl.CostEstimate(flops=2 * 256 * D * COLS, bytes_accessed=16 * 2**20, transcendentals=0),
        name="exchange_out",
    )(oc, dqc, terms, dith, x)


def local(queries, key_vectors, activations, value_weight, attended_grad, doc_ids, shard_plan, round_bits):
    docs = jnp.arange(16, dtype=I32)
    starts = jnp.sum((doc_ids < docs[:, None]).astype(I32), axis=1)
    first = jnp.sum(jnp.where(doc_ids == docs[:, None], starts[:, None], 0), axis=0)
    earlier = (jnp.arange(SEQ, dtype=I32) - first).reshape(SEQ // BLOCK, BLOCK)
    lens = jnp.tile(earlier, (1, GROUP))
    blocks = jnp.arange(SEQ // BLOCK, dtype=I32)
    match = shard_plan[0][:, None] == jnp.arange(128, dtype=I32)[None, :]
    place = jnp.sum(jnp.where(match, blocks[:, None], 0), axis=0)
    plc = jnp.broadcast_to(place[None, :], (8, 128))
    qa, ga, ka, va, lensp, plcp = exchange_in(
        queries[0], attended_grad[0], key_vectors[0], activations[0], value_weight, lens, plc
    )
    bits = round_bits.transpose(0, 2, 1).reshape(N_CTX * 8, SEQ)
    oc, dqc, terms, dith = attend(plcp, qa, ga, ka, va, lensp, bits)
    att, dqo, dko, wg = exchange_out(oc, dqc, terms, dith, activations[0])
    return att[None], dqo[None], dko[None], wg


def solution(mesh):
    rows = P("dp", "ctx", None)
    every = P(("dp", "ctx"), None)
    return jax.shard_map(
        local,
        mesh=mesh,
        in_specs=(rows, rows, rows, every, rows, P("dp", None), P("dp", None), P()),
        out_specs=(rows, rows, rows, every),
        check_vma=False,
    )
```

time: 2310 us -> 193 us (0.08)
  the two profiles are of different devices: /device:TPU:136 before, /device:TPU:1 now
where the time goes in v1:
time: 193 us
  Pallas kernels  176 us (91%)
  local copies, waits for them, and re-layouts  13.8 us (7%)
  other arithmetic  2.34 us (1%)
    pallas_call x1, Pallas kernels, exchange_out(): pl.pallas_call(out_kernel, out_shape=[jax.ShapeDtypeStruct((TOK, D), BF),...  76.1 us
    pallas_call x1, Pallas kernels, exchange_in(): pl.pallas_call(in_kernel, out_shape=[jax.ShapeDtypeStruct((SEQ // 2, GROU...  75.6 us
    pallas_call x1, Pallas kernels, attend(): pl.pallas_call(attention_kernel, grid_spec=pltpu.PrefetchScalarGridSpec(n...  24.5 us
    unnamed x24, local copies, waits for them, and re-layouts  13.6 us

profile of v1, /device:TPU:1, one launch (start us, length us, event | category | flops | bytes accessed | tf_op | source)
XLA Modules:
  0.0 192.9 jit_solution(11138035053244294730)
XLA Ops:
  0.6 0.8 convert_reduce_fusion
  1.4 0.7 select_reduce_fusion.1
  2.2 0.8 select_reduce_fusion
  3.0 0.1 reduce_sum.31
  3.1 0.1 tile.9.lens
  3.2 0.0 copy-start.1
  3.2 1.2 copy-done.1
  4.4 0.0 copy-start.3
  4.4 1.2 copy-done.3
  5.6 0.0 copy-start.4
  5.6 1.2 copy-done.4
  6.8 0.0 copy-start.5
  6.8 0.9 copy-done.5
  7.7 0.0 copy-start.6
  7.7 0.7 copy-done.6
  8.5 75.6 %exchange_in.1 = (bf16[512,1024]{1,0:T(8,128)(2,1)S(1)}, bf16[512,1024]{1,0:T(8,128)(2,1)S(1)}, bf16[1024,128]{1,0:T(8,128)(2,1)S(1)}, bf16[1024,128]{1,0:T(8,12...) custom-call(bf16[128,4096]{1,0:T(8,128)(2,1)S(1)} %bitcast.14, bf16[128,4096]{1,0:T(8,128)(2,1)S(1)} %bitcast.15, ...), custom_call_target="tpu_custom_call" | custom-call | flops 536870912 | bytes 16777216 | tf_op jit(solution)/shard_map/exchange_in/pallas_call | solution.py:215
  84.0 0.0 copy-start.7
  84.0 1.0 copy-done.7
  85.0 0.0 copy-start.8
  85.0 1.0 copy-done.8
  86.0 0.0 copy-start.9
  86.0 0.9 copy-done.9
  86.9 0.0 copy-start.2
  86.9 24.5 %attention.1 = (bf16[512,1024]{1,0:T(8,128)(2,1)S(1)}, bf16[512,1024]{1,0:T(8,128)(2,1)S(1)}, bf16[2,2,8,512,128]{4,3,2,1,0:T(8,128)(2,1)}, f32[512,128]{1,0:T(8,128)S(1)}) custom-call(s32[2,8,128]{2,1,0:T(8,128)S(1)} %get-tuple-element.18.plc, bf16[512,1024]{1,0:T(8,128)(2,1)} %copy-done.7, bf16[512,1024]{1,0:T(8,128)(2,1)} %copy-done.8, ...), custom_call_target="tpu_custom_call" | custom-call | flops 3422552064 | bytes 12582912 | tf_op jit(solution)/shard_map/attention/pallas_call | solution.py:343
  111.5 0.0 copy-done.2
  111.5 0.0 copy-start
  111.5 2.2 %copy-done = bf16[2,2,8,512,128]{4,3,2,1,0:T(8,128)(2,1)S(1)} copy-done((bf16[2,2,8,512,128]{4,3,2,1,0:T(8,128)(2,1)S(1)}, bf16[2,2,8,512,128]{4,3,2,1,0:T(8,128)(2,1)}, u32[]{:S(2)}) %copy-start) | copy-done | bytes 4194328
  113.7 76.1 %exchange_out.1 = (bf16[128,4096]{1,0:T(8,128)(2,1)S(1)}, bf16[128,4096]{1,0:T(8,128)(2,1)S(1)}, bf16[128,512]{1,0:T(8,128)(2,1)S(1)}, f32[16,512]{1,0:T(8,128)S(1)}) custom-call(bf16[512,1024]{1,0:T(8,128)(2,1)S(1)} %get-tuple-element.24.oc, bf16[512,1024]{1,0:T(8,128)(2,1)S(1)} %get-tuple-element.25.dqc, bf16[2,2,8,512,128]{4,3,2,1,0:T(8,128)(2,1)S(1)} %copy-done, ...), custom_call_target="tpu_custom_call" | custom-call | flops 536870912 | bytes 16777216 | tf_op jit(solution)/shard_map/exchange_out/pallas_call | solution.py:505
  189.7 1.0 copy.16
  190.7 1.0 copy.17
  191.7 0.7 copy.18
  192.3 0.6 copy.19
  (3 shorter events, 0.0 us)
Async XLA Ops:
  3.2 1.2 copy-start.1
  4.4 1.2 copy-start.3
  5.6 1.2 copy-start.4
  6.8 0.9 copy-start.5
  7.7 0.7 copy-start.6
  84.0 1.0 copy-start.7
  85.0 1.0 copy-start.8
  86.0 0.9 copy-start.9
  86.9 24.5 %copy-start.2 = (bf16[1,128,4096]{2,1,0:T(8,128)(2,1)S(1)}, bf16[1,128,4096]{2,1,0:T(8,128)(2,1)}, u32[]{:S(2)}) copy-start(bf16[1,128,4096]{2,1,0:T(8,128)(2,1)} %param.10) | copy-start | bytes 3145732
  111.5 2.2 %copy-start = (bf16[2,2,8,512,128]{4,3,2,1,0:T(8,128)(2,1)S(1)}, bf16[2,2,8,512,128]{4,3,2,1,0:T(8,128)(2,1)}, u32[]{:S(2)}) copy-start(bf16[2,2,8,512,128]{4,3,2,1,0:T(8,128)(2,1)} %get-tuple-element.26.terms) | copy-start | bytes 12582916

commit v2 on v1

--- a/solution.py
+++ b/solution.py
@@ -30,6 +30,9 @@
 SCALE = HEAD**-0.5
 LOG2E = 1.4426950408889634
 NEG = -1e30
+SUBS = 2
+SUB_ROWS = 512 // SUBS
+DROWS = 64
 
 
 def vmem(shape, dtype):
@@ -139,22 +142,46 @@
     for n in range(8):
         core, j = n // 4, n % 4
         push(me, k_src(j), ka.at[pl.ds(spot, TOK), :], k_s.at[n], k_r.at[me.ctx], core, me.core * 4 + j)
+    for n in range(16):
+        landed(wfull.at[me.ylo, me.z, pl.ds(n * 16, 16), :], w_r.at[n])
+    mine = wfull.at[me.ylo, me.z]
+    over = remote(mine, mine, one_s.at[3], one_r.at[3], me.across)
+    over.start()
+
+    def piece(z, sub):
+        ylo = me.ylo if sub < SUBS // 2 else 1 - me.ylo
+        return wfull.at[ylo, z, pl.ds(sub % (SUBS // 2) * SUB_ROWS, SUB_ROWS), :]
+
+    def ring(s, sub):
+        z_up, z_dn = (me.z + N_Z - s) % N_Z, (me.z + s) % N_Z
+        n = s * SUBS + sub
+        up = remote(piece(z_up, sub), piece(z_up, sub), up_s.at[n], up_r.at[n], me.up)
+        dn = remote(piece(z_dn, sub), piece(z_dn, sub), dn_s.at[n], dn_r.at[n], me.down)
+        if s < 3:
+            return [up, dn]
+        return [up] if sub % 2 == 0 else [dn]
+
+    started = {}
+
+    def go(s, sub):
+        started[s, sub] = ring(s, sub)
+        for copy in started[s, sub]:
+            copy.start()
+
+    for sub in range(SUBS // 2):
+        go(0, sub)
     for n in range(8):
         core, j = n // 4, n % 4
         push(me, wide(q, core, j), qa.at[pl.ds(half_spot, HALF), :], q_s.at[n], q_r.at[me.ctx], core, me.core * 4 + j)
     for n in range(8):
         core, j = n // 4, n % 4
         push(me, wide(g, core, j), ga.at[pl.ds(half_spot, HALF), :], g_s.at[n], g_r.at[me.ctx], core, me.core * 4 + j)
-
-    for n in range(16):
-        landed(wfull.at[me.ylo, me.z, pl.ds(n * 16, 16), :], w_r.at[n])
-    mine = wfull.at[me.ylo, me.z]
-    over = remote(mine, mine, one_s.at[3], one_r.at[3], me.across)
-    over.start()
     own_x.wait()
     far_x.wait()
     vacc[...] = jnp.zeros_like(vacc)
     over.wait()
+    for sub in range(SUBS // 2, SUBS):
+        go(0, sub)
 
     def project(z):
         for ylo in range(2):
@@ -162,23 +189,19 @@
             part = xv[:, :, pl.ds(col, 256)].reshape(2 * TOK, 256)
             vacc[...] += jnp.dot(part, wfull[ylo, z], preferred_element_type=F32)
 
-    def chunk(z):
-        return wfull.at[:, z]
-
-    for s in range(4):
-        z_up = (me.z + N_Z - s) % N_Z
-        up = remote(chunk(z_up), chunk(z_up), up_s.at[s], up_r.at[s], me.up)
-        up.start()
-        if s < 3:
-            z_dn = (me.z + s) % N_Z
-            dn = remote(chunk(z_dn), chunk(z_dn), dn_s.at[s], dn_r.at[s], me.down)
-            dn.start()
-        project(z_up)
-        if s > 0:
-            project((me.z + s) % N_Z)
-        up.wait()
-        if s < 3:
-            dn.wait()
+    for s in range(1, 4):
+        for sub in range(SUBS):
+            up, dn = started[s - 1, sub]
+            up.wait_recv()
+            dn.wait_recv()
+            go(s, sub)
+        project((me.z + N_Z - s + 1) % N_Z)
+        if s > 1:
+            project((me.z + s - 1) % N_Z)
+    project((me.z + N_Z - 3) % N_Z)
+    project((me.z + 3) % N_Z)
+    for sub in range(SUBS):
+        started[3, sub][0].wait_recv()
     project((me.z + N_Z - 4) % N_Z)
 
     vbuf[...] = vacc[...].astype(BF)
@@ -193,6 +216,9 @@
             par * 4 + me.core * 2 + jj,
         )
 
+    for copies in started.values():
+        for copy in copies:
+            copy.wait_send()
     for n, (core, ctx) in enumerate(plane):
         pushed(me, w_src(core), w_s.at[n], core, ctx)
     for n in range(8):
@@ -227,10 +253,10 @@
         scratch_shapes=[
             vmem((2, N_Z, 256, COLS), BF), vmem((2, TOK, D), BF), vmem((2 * TOK, COLS), BF), vmem((2 * TOK, COLS), F32),
             dma(16), dma(16), dma(8), dma(8), dma(8), dma(8), dma(8), dma(8), dma(8), dma(8),
-            dma(4), dma(4), dma(4), dma(4), dma(3), dma(3), dma(3),
+            dma(4), dma(4), dma(4 * SUBS), dma(4 * SUBS), dma(4 * SUBS), dma(4 * SUBS), dma(3),
         ],
         compiler_params=pltpu.CompilerParams(
-            collective_id=0, has_side_effects=True, vmem_limit_bytes=24 * 2**20
+            collective_id=0, has_side_effects=True, vmem_limit_bytes=60 * 2**20
         ),
         cost_estimate=pl.CostEstimate(flops=2 * 256 * D * COLS, bytes_accessed=16 * 2**20, transcendentals=0),
         name="exchange_in",
@@ -359,7 +385,7 @@
             jax.ShapeDtypeStruct((2, 2, N_CTX, SEQ // 2, HEAD), BF),
             jax.ShapeDtypeStruct((SEQ // 2, HEAD), F32),
         ],
-        compiler_params=pltpu.CompilerParams(vmem_limit_bytes=50 * 2**20),
+        compiler_params=pltpu.CompilerParams(vmem_limit_bytes=60 * 2**20),
         cost_estimate=pl.CostEstimate(
             flops=12 * 16 * 256 * WIN * HEAD, bytes_accessed=12 * 2**20, transcendentals=16 * 256 * WIN
         ),
@@ -370,67 +396,64 @@
 def out_kernel(
     oc, dqc, terms, dith, x, att, dqo, dko, wg,
     xv, own, part, dv_pair, kd, vd, jit, up_b, dn_b, up_in, dn_in, y_b, y_in, c_b, c_in, wsum,
-    o_s, o_r, d_s, d_r, dk_s, dk_r, dv_s, dv_r, one_s, one_r, up_s, up_r, dn_s, dn_r, c_s, c_r, loc,
+    sw_s, sw_r, ke_s, o_s, o_r, d_s, d_r, dk_s, dk_r, dv_s, dv_r, one_s, one_r, up_s, up_r, dn_s, dn_r, c_s, c_r, loc,
 ):
     me = Place()
     greet(me)
     away = 1 - me.core
-    swap = remote(terms.at[away], part, one_s.at[0], one_r.at[0], me.partner)
-    swap.start()
-    keep = pltpu.make_async_copy(terms.at[me.core], own, loc.at[0])
-    keep.start()
-    jit_in = pltpu.make_async_copy(dith, jit, loc.at[1])
+    def rows_of(n):
+        return pl.ds(n * TOK, TOK)
+
+    swaps, keeps = [], []
+    for n in range(4):
+        src, dst = terms.at[away, :, :, rows_of(n), :], part.at[:, :, rows_of(n), :]
+        swaps.append(remote(src, dst, sw_s.at[n], sw_r.at[n], me.partner))
+        keeps.append(
+            pltpu.make_async_copy(terms.at[me.core, :, :, rows_of(n), :], own.at[:, :, rows_of(n), :], ke_s.at[n])
+        )
+    jit_in = pltpu.make_async_copy(dith, jit, loc.at[0])
+    far_x = remote(x, xv.at[me.core], one_s.at[1], one_r.at[1], me.partner)
+    own_x = pltpu.make_async_copy(x, xv.at[me.core], loc.at[1])
     jit_in.start()
-    far_x = remote(x, xv.at[me.core], one_s.at[1], one_r.at[1], me.partner)
+    for n in range(4):
+        swaps[n].start()
+        keeps[n].start()
     far_x.start()
-    own_x = pltpu.make_async_copy(x, xv.at[me.core], loc.at[2])
     own_x.start()
 
-    def wide(ref, j):
-        return ref.at[pl.ds(pl.multiple_of(me.core * HALF, HALF), HALF), pl.ds(pl.multiple_of(j * GROUP * HEAD, HEAD), GROUP * HEAD)]
-
-    def home(ref, i):
-        return ref.at[pl.ds(i * HALF, HALF), :]
-
-    for src, dst, ssem, rsem in ((oc, att, o_s, o_r), (dqc, dqo, d_s, d_r)):
-        for i in range(N_CTX):
-            push(me, home(src, i), wide(dst, me.head), ssem.at[i], rsem.at[me.core * 4 + me.head], me.par, i)
-
-    swap.wait()
-    keep.wait()
-    jit_in.wait()
-
-    @pl.loop(0, 16)
-    def _(n):
-        rows = pl.ds(pl.multiple_of(n * BLOCK, BLOCK), BLOCK)
-        noise = jit[rows, :]
-        for f, out in ((0, kd), (1, vd)):
-            acc = jnp.zeros((BLOCK, HEAD), F32)
-            for t in range(N_CTX):
-                total = acc + own[f, t, rows, :].astype(F32) + part[f, t, rows, :].astype(F32)
-                u = noise[:, f * 8 + t : f * 8 + t + 1]
-                acc = (total + u * jnp.abs(total)).astype(BF).astype(F32)
-            out[rows, :] = acc.astype(BF)
-
     def tile(ref, n):
-        return ref.at[pl.ds(n * TOK, TOK), :]
+        return ref.at[rows_of(n), :]
 
     v_core = me.head // 2
     v_col = pl.multiple_of(me.head % 2 * HEAD, HEAD)
+    k_col = pl.multiple_of(me.head * HEAD, HEAD)
+    v_dst = dv_pair.at[pl.ds(pl.multiple_of(me.par * TOK, TOK), TOK), pl.ds(v_col, HEAD)]
+    k_dst = dko.at[:, pl.ds(k_col, HEAD)]
+    jit_in.wait()
     for n in range(4):
-        push(
-            me, tile(vd, n), dv_pair.at[pl.ds(pl.multiple_of(me.par * TOK, TOK), TOK), pl.ds(v_col, HEAD)],
-            dv_s.at[n], dv_r.at[me.par * 2 + me.head % 2], v_core, me.core * 4 + n,
-        )
-    k_col = pl.multiple_of(me.head * HEAD, HEAD)
-    for n in range(4):
-        push(
-            me, tile(kd, n), dko.at[:, pl.ds(k_col, HEAD)], dk_s.at[n], dk_r.at[me.head], me.par, me.core * 4 + n
-        )
+        swaps[n].wait_recv()
+        keeps[n].wait()
+
+        @pl.loop(0, TOK // DROWS)
+        def _(m, n=n):
+            rows = pl.ds(pl.multiple_of(n * TOK + m * DROWS, DROWS), DROWS)
+            noise = jit[rows, :]
+            for f, out in ((0, kd), (1, vd)):
+                acc = jnp.zeros((DROWS, HEAD), F32)
+                for t in range(N_CTX):
+                    total = acc + (own[f, t, rows, :].astype(F32) + part[f, t, rows, :].astype(F32))
+                    u = noise[:, f * 8 + t : f * 8 + t + 1]
+                    acc = (total + u * jnp.abs(total)).astype(BF).astype(F32)
+                out[rows, :] = acc.astype(BF)
+
+        push(me, tile(vd, n), v_dst, dv_s.at[n], dv_r.at[me.par * 2 + me.head % 2], v_core, me.core * 4 + n)
     own_x.wait()
     far_x.wait()
     for n in range(4):
         landed(dv_pair.at[pl.ds(n // 2 * TOK, TOK), pl.ds(n % 2 * HEAD, HEAD)], dv_r.at[n])
+
+    def sub_ylo(sub):
+        return 1 - me.ylo if sub == 0 else me.ylo
 
     def local_sum(z, ylo):
         col = pl.multiple_of(ylo * 2048 + z * 256, 256)
@@ -438,39 +461,60 @@
             xv[:, :, pl.ds(col, 256)].reshape(2 * TOK, 256), dv_pair[...], TN, preferred_element_type=F32
         )
 
-    for s in range(4):
-        z_up = (me.z + 4 - s) % N_Z
-        for ylo in range(2):
-            total = local_sum(z_up, ylo)
-            if s > 0:
-                total = total + up_in[s - 1, ylo].astype(F32)
-            up_b[s, ylo] = total.astype(BF)
-        up = remote(up_b.at[s], up_in.at[s], up_s.at[s], up_r.at[s], me.up)
-        up.start()
-        if s < 3:
-            z_dn = (me.z + N_Z - 3 + s) % N_Z
-            for ylo in range(2):
-                total = local_sum(z_dn, ylo)
-                if s > 0:
-                    total = total + dn_in[s - 1, ylo].astype(F32)
-                dn_b[s, ylo] = total.astype(BF)
-            dn = remote(dn_b.at[s], dn_in.at[s], dn_s.at[s], dn_r.at[s], me.down)
-            dn.start()
-        if s == 3:
-            for ylo in range(2):
-                wsum[ylo] = local_sum(me.z, ylo) + dn_in[2, ylo].astype(F32)
-        up.wait()
-        if s < 3:
-            dn.wait()
-    for ylo in range(2):
-        wsum[ylo] += up_in[3, ylo].astype(F32)
-
-    y_b[...] = wsum[1 - me.ylo].astype(BF)
+    ways = ((1, up_b, up_in, up_s, up_r, me.up), (-1, dn_b, dn_in, dn_s, dn_r, me.down))
+
+    def ring(w, s, sub):
+        _, buf, inn, ssem, rsem, to = ways[w]
+        n = s * 2 + sub
+        return remote(buf.at[n], inn.at[n], ssem.at[n], rsem.at[n], to)
+
+    started = {}
+
+    def go(w, s, sub):
+        sign, buf, inn = ways[w][:3]
+        n = s * 2 + sub
+        total = local_sum((me.z + N_Z + sign * (4 - s)) % N_Z, sub_ylo(sub))
+        if (w, s - 1, sub) in started:
+            started[w, s - 1, sub].wait_recv()
+            total = total + inn[n - 2].astype(F32)
+        buf[n] = total.astype(BF)
+        started[w, s, sub] = ring(w, s, sub)
+        started[w, s, sub].start()
+
+    go(0, 0, 0)
+    go(1, 0, 1)
+
+    def wide(ref, j):
+        cols = pl.ds(pl.multiple_of(j * GROUP * HEAD, HEAD), GROUP * HEAD)
+        return ref.at[pl.ds(pl.multiple_of(me.core * HALF, HALF), HALF), cols]
+
+    def home(ref, i):
+        return ref.at[pl.ds(i * HALF, HALF), :]
+
+    for src, dst, ssem, rsem in ((oc, att, o_s, o_r), (dqc, dqo, d_s, d_r)):
+        for i in range(N_CTX):
+            push(me, home(src, i), wide(dst, me.head), ssem.at[i], rsem.at[me.core * 4 + me.head], me.par, i)
+    for n in range(4):
+        push(me, tile(kd, n), k_dst, dk_s.at[n], dk_r.at[me.head], me.par, me.core * 4 + n)
+
+    for s in range(1, 4):
+        for sub in range(2):
+            go(0, s, sub)
+            go(1, s, sub)
+
+    def finish(sub):
+        total = local_sum(me.z, sub_ylo(sub))
+        for w in range(2):
+            started[w, 3, sub].wait_recv()
+            total = total + ways[w][2][6 + sub].astype(F32)
+        return total
+
+    y_b[...] = finish(0).astype(BF)
     over = remote(y_b, y_in, one_s.at[2], one_r.at[2], me.across)
     over.start()
+    wsum[...] = finish(1)
     over.wait()
-    c_b[...] = (wsum[me.ylo] + y_in[...].astype(F32)).astype(BF)
-
+    c_b[...] = (wsum[...] + y_in[...].astype(F32)).astype(BF)
     for n in range(16):
         push(
             me, c_b.at[pl.ds(n * 16, 16), :], c_in.at[me.core, me.ctx], c_s.at[n], c_r.at[me.core * N_CTX + me.ctx],
@@ -484,6 +528,10 @@
             total = total + c_in[core, i].astype(F32)
         wg[:, core * COLS : (core + 1) * COLS] = total
 
+    for n in range(4):
+        swaps[n].wait_send()
+    for copy in started.values():
+        copy.wait_send()
     for n in range(16):
         pushed(me, c_b.at[pl.ds(n * 16, 16), :], c_s.at[n], n // N_CTX, n % N_CTX)
     for n in range(4):
@@ -501,7 +549,7 @@
 
 
 def exchange_out(oc, dqc, terms, dith, x):
-    slab = (2, 256, COLS)
+    slab = (256, COLS)
     return pl.pallas_call(
         out_kernel,
         out_shape=[
@@ -515,14 +563,14 @@
         scratch_shapes=[
             vmem((2, TOK, D), BF), vmem((2, N_CTX, SEQ // 2, HEAD), BF), vmem((2, N_CTX, SEQ // 2, HEAD), BF),
             vmem((2 * TOK, COLS), BF), vmem((SEQ // 2, HEAD), BF), vmem((SEQ // 2, HEAD), BF), vmem((SEQ // 2, HEAD), F32),
-            vmem((4,) + slab, BF), vmem((3,) + slab, BF), vmem((4,) + slab, BF), vmem((3,) + slab, BF),
-            vmem((256, COLS), BF), vmem((256, COLS), BF), vmem((256, COLS), BF), vmem((2, N_CTX, 16, COLS), BF),
-            vmem(slab, F32),
+            vmem((8,) + slab, BF), vmem((8,) + slab, BF), vmem((8,) + slab, BF), vmem((8,) + slab, BF),
+            vmem(slab, BF), vmem(slab, BF), vmem(slab, BF), vmem((2, N_CTX, 16, COLS), BF), vmem(slab, F32),
+            dma(4), dma(4), dma(4),
             dma(8), dma(8), dma(8), dma(8), dma(4), dma(4), dma(4), dma(4), dma(3), dma(3),
-            dma(4), dma(4), dma(3), dma(3), dma(16), dma(16), dma(3),
+            dma(8), dma(8), dma(8), dma(8), dma(16), dma(16), dma(2),
         ],
         compiler_params=pltpu.CompilerParams(
-            collective_id=1, has_side_effects=True, vmem_limit_bytes=32 * 2**20
+            collective_id=1, has_side_effects=True, vmem_limit_bytes=60 * 2**20
         ),
         cost_estimate=pl.CostEstimate(flops=2 * 256 * D * COLS, bytes_accessed=16 * 2**20, transcendentals=0),
         name="exchange_out",

time: 193 us -> 140 us (0.73)
  Pallas kernels: 176 us -> 129 us
  local copies, waits for them, and re-layouts: 13.8 us -> 7.28 us
    pallas_call x1, Pallas kernels: 76.1 us -> 47.9 us  [exchange_out(): pl.pallas_call(out_kernel, out_shape=[jax.ShapeDtypeStruct((TOK, D), BF),...]
    pallas_call x1, Pallas kernels: 75.6 us -> 55.5 us  [exchange_in(): pl.pallas_call(in_kernel, out_shape=[jax.ShapeDtypeStruct((SEQ // 2, GROU...]
    unnamed x24 -> x8, local copies, waits for them, and re-layouts: 13.6 us -> 5.89 us
where the time goes in v2:
time: 140 us; the launch traced here: 139 us
  Pallas kernels  129 us (92%)
  local copies, waits for them, and re-layouts  7.28 us (5%)
  other arithmetic  2.34 us (2%)
    pallas_call x1, Pallas kernels, exchange_in(): pl.pallas_call(in_kernel, out_shape=[jax.ShapeDtypeStruct((SEQ // 2, GROU...  55.5 us
    pallas_call x1, Pallas kernels, exchange_out(): pl.pallas_call(out_kernel, out_shape=[jax.ShapeDtypeStruct((TOK, D), BF),...  47.9 us
    pallas_call x1, Pallas kernels, attend(): pl.pallas_call(attention_kernel, grid_spec=pltpu.PrefetchScalarGridSpec(n...  25.4 us
    unnamed x8, local copies, waits for them, and re-layouts  5.89 us

profile of v2, /device:TPU:1, one launch (start us, length us, event | category | flops | bytes accessed | tf_op | source)
XLA Modules:
  0.0 139.0 jit_solution(9861833187462448941)
XLA Ops:
  0.6 0.8 convert_reduce_fusion
  1.4 0.7 select_reduce_fusion.1
  2.2 0.6 broadcast_in_dim.48.plc
  2.8 0.8 select_reduce_fusion
  3.6 0.1 reduce_sum.31
  3.7 0.7 tile.9.lens
  4.4 55.5 %exchange_in.1 = (bf16[512,1024]{1,0:T(8,128)(2,1)}, bf16[512,1024]{1,0:T(8,128)(2,1)}, bf16[1024,128]{1,0:T(8,128)(2,1)}, bf16[1024,128]{1,0:T(8,128)(2,1)}, s3...) custom-call(bf16[128,4096]{1,0:T(8,128)(2,1)} %bitcast.14, bf16[128,4096]{1,0:T(8,128)(2,1)} %bitcast.15, ...), custom_call_target="tpu_custom_call" | custom-call | flops 536870912 | bytes 16777216 | tf_op jit(solution)/shard_map/exchange_in/pallas_call | solution.py:241
  59.8 25.4 %attention.1 = (bf16[512,1024]{1,0:T(8,128)(2,1)}, bf16[512,1024]{1,0:T(8,128)(2,1)}, bf16[2,2,8,512,128]{4,3,2,1,0:T(8,128)(2,1)}, f32[512,128]{1,0:T(8,128)}) custom-call(s32[2,8,128]{2,1,0:T(8,128)} %get-tuple-element.18.plc, bf16[512,1024]{1,0:T(8,128)(2,1)} %get-tuple-element.19.q, bf16[512,1024]{1,0:T(8,128)(2,1)} %get-tuple-element.20.g, ...), custom_call_target="tpu_custom_call" | custom-call | flops 3422552064 | bytes 12582912 | tf_op jit(solution)/shard_map/attention/pallas_call | solution.py:369
  85.2 47.9 %exchange_out.1 = (bf16[128,4096]{1,0:T(8,128)(2,1)}, bf16[128,4096]{1,0:T(8,128)(2,1)}, bf16[128,512]{1,0:T(8,128)(2,1)}, f32[16,512]{1,0:T(8,128)}) custom-call(bf16[512,1024]{1,0:T(8,128)(2,1)} %get-tuple-element.24.oc, bf16[512,1024]{1,0:T(8,128)(2,1)} %get-tuple-element.25.dqc, bf16[2,2,8,512,128]{4,3,2,1,0:T(8,128)(2,1)} %get-tuple-element.26.terms, ...), custom_call_target="tpu_custom_call" | custom-call | flops 536870912 | bytes 16777216 | tf_op jit(solution)/shard_map/exchange_out/pallas_call | solution.py:553
  133.1 0.0 copy-start
  133.1 0.0 copy-start.1
  133.1 2.3 %copy.16 = bf16[1,128,4096]{2,1,0:T(8,128)(2,1)} copy(bf16[1,128,4096]{2,1,0:T(8,128)(2,1)} %bitcast.17) | data formatting | bytes 2097152
  135.5 2.3 %copy.17 = bf16[1,128,4096]{2,1,0:T(8,128)(2,1)} copy(bf16[1,128,4096]{2,1,0:T(8,128)(2,1)} %bitcast.16) | data formatting | bytes 2097152
  137.8 0.0 copy-done
  137.8 0.7 copy.18
  138.4 0.0 copy-done.1
  138.4 0.6 copy.19
  (2 shorter events, 0.0 us)
Async XLA Ops:
  133.1 4.6 %copy-start = (bf16[128,512]{1,0:T(8,128)(2,1)S(1)}, bf16[128,512]{1,0:T(8,128)(2,1)}, u32[]{:S(2)}) copy-start(bf16[128,512]{1,0:T(8,128)(2,1)} %get-tuple-element.30) | copy-start | bytes 393220
  133.1 5.3 %copy-start.1 = (f32[16,512]{1,0:T(8,128)S(1)}, f32[16,512]{1,0:T(8,128)}, u32[]{:S(2)}) copy-start(f32[16,512]{1,0:T(8,128)} %get-tuple-element.39) | copy-start | bytes 98308

commit v3 on v2

v3 whole, which is shorter than its diff:
```python
import functools

import jax
import jax.numpy as jnp
from jax import lax
from jax.experimental import pallas as pl
from jax.experimental.pallas import tpu as pltpu
from jax.sharding import PartitionSpec as P

MESH = pl.DeviceIdType.MESH
ANY = pl.BlockSpec(memory_space=pl.ANY)
BF = jnp.bfloat16
F32 = jnp.float32
I32 = jnp.int32

N_CTX = 8
N_Z = 8
HEAD = 128
GROUP = 8
TOK = 128
HALF = 64
SEQ = 1024
BLOCK = 32
BAND = 512
WIN = BAND + BLOCK
D = 4096
KVW = 512
COLS = 256
PAD_ROWS = SEQ + BAND + 128
SCALE = HEAD**-0.5
LOG2E = 1.4426950408889634
NEG = -1e30
SUBS = 2
SUB_ROWS = 512 // SUBS
DROWS = 64
EDGE = 3 * BLOCK
SPAN = WIN + 2 * EDGE
CAND = 12

NT = (((1,), (1,)), ((), ()))
TN = (((0,), (0,)), ((), ()))


def vmem(shape, dtype):
    return pltpu.VMEM(shape, dtype)


def dma(*shape):
    return pltpu.SemaphoreType.DMA(shape)


class Place:
    def __init__(self):
        self.dp = lax.axis_index("dp")
        self.ctx = lax.axis_index("ctx")
        self.core = self.dp % 2
        self.z = (self.dp // 2) % N_Z
        self.ylo = self.dp // 16
        self.base = self.dp - self.core
        self.par = self.ctx // 4
        self.head = self.ctx % 4
        self.partner = (self.base + 1 - self.core, self.ctx)
        self.across = (self.dp + 16 - 32 * self.ylo, self.ctx)
        self.up = (self.ylo * 16 + (self.z + 1) % N_Z * 2 + self.core, self.ctx)
        self.down = (self.ylo * 16 + (self.z + N_Z - 1) % N_Z * 2 + self.core, self.ctx)

    def is_me(self, core, ctx):
        return (self.core == core) & (self.ctx == ctx)


def greet(me):
    barrier = pltpu.get_barrier_semaphore()
    for core in range(2):
        for ctx in range(N_CTX):

            @pl.when(jnp.logical_not(me.is_me(core, ctx)))
            def _(core=core, ctx=ctx):
                pl.semaphore_signal(barrier, inc=1, device_id=(me.base + core, jnp.int32(ctx)), device_id_type=MESH)

    for other in (me.across, me.up, me.down):
        pl.semaphore_signal(barrier, inc=1, device_id=other, device_id_type=MESH)
    pl.semaphore_wait(barrier, 2 * N_CTX + 2)


def remote(src, dst, ssem, rsem, device):
    return pltpu.make_async_remote_copy(
        src_ref=src, dst_ref=dst, send_sem=ssem, recv_sem=rsem, device_id=device, device_id_type=MESH
    )


def push(me, src, dst, ssem, rsem, core, ctx):
    mine = me.is_me(core, ctx)

    @pl.when(mine)
    def _():
        pltpu.make_async_copy(src, dst, rsem).start()

    @pl.when(jnp.logical_not(mine))
    def _():
        remote(src, dst, ssem, rsem, (me.base + core, jnp.int32(ctx))).start()


def pushed(me, src, ssem, core, ctx):
    @pl.when(jnp.logical_not(me.is_me(core, ctx)))
    def _():
        remote(src, src, ssem, ssem, (me.base + core, jnp.int32(ctx))).wait_send()


def landed(dst, rsem):
    pltpu.make_async_copy(dst, dst, rsem).wait()


def kernel(
    q, g, k, x, w, lens, plc, tsel, bits, att, dqo, dko, wg,
    wfull, xv, vbuf, vacc, qa, ga, oc, dqc, kpad, vpad, kt, vt, lensv, plcv, bitv, jit,
    tsv, code, pst, kvb, away_t, own_t, part, dv_pair, kd, vd,
    up_b, dn_b, up_in, dn_in, y_b, y_in, c_b, c_in, wsum,
    w_s, w_r, q_s, q_r, g_s, g_r, k_s, k_r, v_s, v_r, one_s, one_r, up_s, up_r, dn_s, dn_r, loc,
    sw_s, sw_r, o_s, o_r, d_s, d_r, dk_s, dk_r, dv_s, dv_r, ru_s, ru_r, rd_s, rd_r, c_s, c_r,
):
    me = Place()
    core, par = me.core, me.par
    for pad in (kpad, vpad):
        pad[0:BAND, :] = jnp.zeros((BAND, HEAD), BF)
        pad[BAND + SEQ :, :] = jnp.zeros((PAD_ROWS - BAND - SEQ, HEAD), BF)
    kvb[:, 0:EDGE, :] = jnp.zeros((16, EDGE, 2 * HEAD), BF)
    kvb[:, EDGE + WIN :, :] = jnp.zeros((16, EDGE, 2 * HEAD), BF)
    down = lax.broadcasted_iota(I32, code.shape, 0)
    right = lax.broadcasted_iota(I32, code.shape, 1)
    code[...] = jnp.where(down % BLOCK == right % BLOCK, down // BLOCK, N_CTX)
    vacc[...] = jnp.zeros_like(vacc)
    greet(me)
    plane = [(n // N_CTX, n % N_CTX) for n in range(2 * N_CTX)]

    def w_src(core):
        return w.at[:, pl.ds(core * COLS, COLS)]

    row = pl.multiple_of(me.core * 128 + me.ctx * 16, 16)
    w_dst = wfull.at[me.ylo, me.z, pl.ds(row, 16), :]
    for n, (to, ctx) in enumerate(plane):
        push(me, w_src(to), w_dst, w_s.at[n], w_r.at[me.core * N_CTX + me.ctx], to, ctx)

    own_x = pltpu.make_async_copy(x, xv.at[me.core], loc.at[0])
    own_l = pltpu.make_async_copy(lens, lensv.at[me.core], loc.at[1])
    own_p = pltpu.make_async_copy(plc, plcv.at[me.core], loc.at[2])
    far_x = remote(x, xv.at[me.core], one_s.at[0], one_r.at[0], me.partner)
    far_l = remote(lens, lensv.at[me.core], one_s.at[1], one_r.at[1], me.partner)
    far_p = remote(plc, plcv.at[me.core], one_s.at[2], one_r.at[2], me.partner)
    own_t_sel = pltpu.make_async_copy(tsel.at[me.core], tsv.at[me.core], loc.at[4])
    far_t_sel = remote(tsel.at[1 - me.core], tsv.at[me.core], one_s.at[4], one_r.at[4], me.partner)
    bits_in = pltpu.make_async_copy(bits, bitv, loc.at[3])
    for copy in (own_x, far_x, own_l, far_l, own_p, far_p, own_t_sel, far_t_sel, bits_in):
        copy.start()

    def k_src(j):
        return k.at[:, pl.ds(j * HEAD, HEAD)]

    def wide(ref, core, j):
        return ref.at[pl.ds(core * HALF, HALF), pl.ds(j * GROUP * HEAD, GROUP * HEAD)]

    spot = pl.multiple_of(BAND + me.ctx * TOK, TOK)
    half_spot = pl.multiple_of(me.ctx * HALF, HALF)

    for n in range(8):
        to, j = n // 4, n % 4
        push(me, k_src(j), kpad.at[pl.ds(spot, TOK), :], k_s.at[n], k_r.at[me.ctx], to, me.core * 4 + j)
    for n in range(16):
        landed(wfull.at[me.ylo, me.z, pl.ds(n * 16, 16), :], w_r.at[n])
    mine = wfull.at[me.ylo, me.z]
    over = remote(mine, mine, one_s.at[3], one_r.at[3], me.across)
    over.start()

    def piece(z, sub):
        ylo = me.ylo if sub < SUBS // 2 else 1 - me.ylo
        return wfull.at[ylo, z, pl.ds(sub % (SUBS // 2) * SUB_ROWS, SUB_ROWS), :]

    def ring(s, sub):
        z_up, z_dn = (me.z + N_Z - s) % N_Z, (me.z + s) % N_Z
        n = s * SUBS + sub
        up = remote(piece(z_up, sub), piece(z_up, sub), up_s.at[n], up_r.at[n], me.up)
        dn = remote(piece(z_dn, sub), piece(z_dn, sub), dn_s.at[n], dn_r.at[n], me.down)
        half = up if sub % 2 == 0 else dn
        return [up, dn] if s < 3 else [half]

    started = {}

    def go(s, sub):
        started[s, sub] = ring(s, sub)
        for copy in started[s, sub]:
            copy.start()

    for sub in range(SUBS // 2):
        go(0, sub)
    for n in range(8):
        to, j = n // 4, n % 4
        push(me, wide(q, to, j), qa.at[pl.ds(half_spot, HALF), :], q_s.at[n], q_r.at[me.ctx], to, me.core * 4 + j)
    for n in range(8):
        to, j = n // 4, n % 4
        push(me, wide(g, to, j), ga.at[pl.ds(half_spot, HALF), :], g_s.at[n], g_r.at[me.ctx], to, me.core * 4 + j)
    own_x.wait()
    far_x.wait()
    over.wait()
    for sub in range(SUBS // 2, SUBS):
        go(0, sub)

    def project(z):
        for ylo in range(2):
            col = pl.multiple_of(ylo * 2048 + z * 256, 256)
            part = xv[:, :, pl.ds(col, 256)].reshape(2 * TOK, 256)
            vacc[...] += jnp.dot(part, wfull[ylo, z], preferred_element_type=F32)

    def transposed(out, pad):
        for b in range(2):
            for n in range(12):
                rows = pl.ds(pl.multiple_of(core * HALF + b * BLOCK + n * 128, BLOCK), 128)
                out[b, :, n * 128 : n * 128 + 128] = pad[rows, :].T

    def stacked(ref, i, b):
        rows = pl.ds(pl.multiple_of(i * HALF + b * BLOCK, BLOCK), BLOCK)
        return jnp.concatenate([ref[rows, h * HEAD : (h + 1) * HEAD] for h in range(GROUP)], axis=0)

    def unstack(ref, i, b, value):
        rows = pl.ds(pl.multiple_of(i * HALF + b * BLOCK, BLOCK), BLOCK)
        for h in range(GROUP):
            ref[rows, h * HEAD : (h + 1) * HEAD] = value[h * BLOCK : (h + 1) * BLOCK]

    def keys_of(i, b):
        block = i * 4 + core * 2 + b
        return block, pl.ds(pl.multiple_of(block * BLOCK, BLOCK), WIN)

    key_row = lax.broadcasted_iota(I32, (WIN, GROUP * BLOCK), 0)
    lane = lax.broadcasted_iota(I32, (1, GROUP * BLOCK), 1) % BLOCK

    def scores(low, high):
        @pl.loop(low, high)
        def _(i):
            landed(qa.at[pl.ds(pl.multiple_of(i * HALF, HALF), HALF), :], q_r.at[i])
            for b in range(2):
                block, rows = keys_of(i, b)
                first = lane + BAND - lensv[par, pl.ds(block, 1), :]
                allowed = (key_row >= first) & (key_row <= lane + BAND)
                s = lax.dot_general(kpad[rows, :], stacked(qa, i, b), NT, preferred_element_type=F32)
                s = jnp.where(allowed, s * (SCALE * LOG2E), NEG)
                weight = jnp.exp2(s - jnp.max(s, axis=0, keepdims=True))
                prob = weight * (1.0 / jnp.sum(weight, axis=0, keepdims=True))
                pst[i * 2 + b] = prob.astype(BF)

    for s in range(1, 4):
        for sub in range(SUBS):
            up, dn = started[s - 1, sub]
            up.wait_recv()
            dn.wait_recv()
            go(s, sub)
        project((me.z + N_Z - s + 1) % N_Z)
        if s > 1:
            project((me.z + s - 1) % N_Z)
    for i in range(N_CTX):
        landed(kpad.at[pl.ds(BAND + i * TOK, TOK), :], k_r.at[i])
    transposed(kt, kpad)
    for copy in (own_l, far_l, own_p, far_p, own_t_sel, far_t_sel):
        copy.wait()
    project((me.z + N_Z - 3) % N_Z)
    project((me.z + 3) % N_Z)
    scores(0, 3)
    for sub in range(SUBS):
        started[3, sub][0].wait_recv()
    project((me.z + N_Z - 4) % N_Z)

    vbuf[...] = vacc[...].astype(BF)

    def v_src(p, jj):
        return vbuf.at[pl.ds(p * TOK, TOK), pl.ds(jj * HEAD, HEAD)]

    routes = [(n // 4, n // 2 % 2, n % 2) for n in range(8)]
    for n, (to, p, jj) in enumerate(routes):
        push(
            me, v_src(p, jj), vpad.at[pl.ds(spot, TOK), :], v_s.at[n], v_r.at[me.ctx], to, p * 4 + me.core * 2 + jj
        )
    scores(3, N_CTX)
    bits_in.wait()
    wanted = [bitv[pl.ds(t * 8 + f * 4 + me.head, 1), :] for f in range(2) for t in range(N_CTX)]
    jitter = (jnp.concatenate(wanted, axis=0).astype(F32) * 2.0**-30 - 0.5) * 2.0**-4
    parts = []
    for _ in range(3):
        parts.append(jitter.astype(BF))
        jitter = jitter - parts[-1].astype(F32)
    at = plcv[par, 0:1, pl.ds(pl.multiple_of(core * (SEQ // 2), SEQ // 2), SEQ // 2)]
    there = lax.broadcasted_iota(I32, (SEQ, SEQ // 2), 0) == at
    moved = jnp.dot(
        jnp.concatenate(parts, axis=0), jnp.where(there, 1.0, 0.0).astype(BF), preferred_element_type=F32
    )
    moved = moved[0:16] + moved[16:32] + moved[32:48]
    jit[...] = jnp.concatenate([moved, jnp.zeros((112, SEQ // 2), F32)], axis=0).T
    for i in range(N_CTX):
        landed(vpad.at[pl.ds(BAND + i * TOK, TOK), :], v_r.at[i])
    transposed(vt, vpad)

    def out_wide(ref, j):
        cols = pl.ds(pl.multiple_of(j * GROUP * HEAD, HEAD), GROUP * HEAD)
        return ref.at[pl.ds(pl.multiple_of(me.core * HALF, HALF), HALF), cols]

    def home(ref, i):
        return ref.at[pl.ds(pl.multiple_of(i * HALF, HALF), HALF), :]

    @pl.loop(0, N_CTX)
    def _(i):
        landed(home(ga, i), g_r.at[i])
        window = pl.ds(pl.multiple_of(i * TOK, TOK), WIN)
        for b in range(2):
            n = i * 2 + b
            _, rows = keys_of(i, b)
            low, qs, gs = pst[n], stacked(qa, i, b), stacked(ga, i, b)
            out_t = jnp.dot(vt[b, :, window], low, preferred_element_type=F32).astype(BF).astype(F32)
            unstack(oc, i, b, out_t.T.astype(BF))
            delta = jnp.sum(gs.astype(F32).T * out_t, axis=0, keepdims=True)
            dprob = lax.dot_general(vpad[rows, :], gs, NT, preferred_element_type=F32)
            dscore = (low.astype(F32) * (dprob - delta)).astype(BF)
            dq_t = jnp.dot(kt[b, :, window], dscore, preferred_element_type=F32)
            unstack(dqc, i, b, (dq_t * SCALE).T.astype(BF))
            key_term = jnp.dot(dscore, qs, preferred_element_type=F32) * SCALE
            kvb[n, EDGE : EDGE + WIN, 0:HEAD] = key_term.astype(BF)
            kvb[n, EDGE : EDGE + WIN, HEAD:] = jnp.dot(low, gs, preferred_element_type=F32).astype(BF)
        push(me, home(oc, i), out_wide(att, me.head), o_s.at[i], o_r.at[me.core * 4 + me.head], me.par, i)

    def gather(out, half, n):
        tile_at = half * 4 + n

        @pl.loop(0, 4)
        def _(m):
            pieces = []
            for c in range(10):
                i, b = (tile_at + c // 2) % N_CTX, c % 2
                row = EDGE + BAND + (m - c // 2 * 4 - core * 2 - b) * BLOCK
                pieces.append(kvb[i * 2 + b, pl.ds(pl.multiple_of(row, BLOCK), BLOCK), :])
            pieces += pieces[0:2]
            step = tsv[par, pl.ds(tile_at * 4 + m, 1), :]
            pick = jnp.where(code[...] == step, 1.0, 0.0).astype(BF)
            sums = jnp.dot(pick, jnp.concatenate(pieces, axis=0), preferred_element_type=F32).astype(BF)
            dst = pl.ds(pl.multiple_of(n * TOK + m * BLOCK, BLOCK), BLOCK)
            for t in range(N_CTX):
                out[0, t, dst, :] = sums[t * BLOCK : (t + 1) * BLOCK, 0:HEAD]
                out[1, t, dst, :] = sums[t * BLOCK : (t + 1) * BLOCK, HEAD:]

    def rows_of(n):
        return pl.ds(n * TOK, TOK)

    swaps = []
    for n in range(4):
        gather(away_t, 1 - core, n)
        swaps.append(
            remote(away_t.at[:, :, rows_of(n), :], part.at[:, :, rows_of(n), :], sw_s.at[n], sw_r.at[n], me.partner)
        )
        swaps[n].start()

    def tile(ref, n):
        return ref.at[rows_of(n), :]

    v_core = me.head // 2
    v_col = pl.multiple_of(me.head % 2 * HEAD, HEAD)
    k_col = pl.multiple_of(me.head * HEAD, HEAD)
    v_dst = dv_pair.at[pl.ds(pl.multiple_of(me.par * TOK, TOK), TOK), pl.ds(v_col, HEAD)]
    k_dst = dko.at[:, pl.ds(k_col, HEAD)]
    for n in range(4):
        gather(own_t, core, n)
        swaps[n].wait_recv()

        @pl.loop(0, 2)
        def _(m, n=n):
            rows = pl.ds(pl.multiple_of(n * TOK + m * DROWS, DROWS), DROWS)
            noise = jit[rows, :]
            for f, out in ((0, kd), (1, vd)):
                acc = jnp.zeros((DROWS, HEAD), F32)
                for t in range(N_CTX):
                    total = acc + (own_t[f, t, rows, :].astype(F32) + part[f, t, rows, :].astype(F32))
                    u = noise[:, f * 8 + t : f * 8 + t + 1]
                    acc = (total + u * jnp.abs(total)).astype(BF).astype(F32)
                out[rows, :] = acc.astype(BF)

        push(me, tile(vd, n), v_dst, dv_s.at[n], dv_r.at[me.par * 2 + me.head % 2], v_core, me.core * 4 + n)
    for n in range(4):
        landed(dv_pair.at[pl.ds(n // 2 * TOK, TOK), pl.ds(n % 2 * HEAD, HEAD)], dv_r.at[n])

    def sub_ylo(sub):
        return 1 - me.ylo if sub == 0 else me.ylo

    def local_sum(z, ylo):
        col = pl.multiple_of(ylo * 2048 + z * 256, 256)
        return lax.dot_general(
            xv[:, :, pl.ds(col, 256)].reshape(2 * TOK, 256), dv_pair[...], TN, preferred_element_type=F32
        )

    ways = ((1, up_b, up_in, ru_s, ru_r, me.up), (-1, dn_b, dn_in, rd_s, rd_r, me.down))

    def sums(w, s, sub):
        _, buf, inn, ssem, rsem, to = ways[w]
        n = s * 2 + sub
        return remote(buf.at[n], inn.at[n], ssem.at[n], rsem.at[n], to)

    travel = {}

    def step(w, s, sub):
        sign, buf, inn = ways[w][:3]
        n = s * 2 + sub
        total = local_sum((me.z + N_Z + sign * (4 - s)) % N_Z, sub_ylo(sub))
        if (w, s - 1, sub) in travel:
            travel[w, s - 1, sub].wait_recv()
            total = total + inn[n - 2].astype(F32)
        buf[n] = total.astype(BF)
        travel[w, s, sub] = sums(w, s, sub)
        travel[w, s, sub].start()

    step(0, 0, 0)
    step(1, 0, 1)

    for i in range(N_CTX):
        push(me, home(dqc, i), out_wide(dqo, me.head), d_s.at[i], d_r.at[me.core * 4 + me.head], me.par, i)
    for n in range(4):
        push(me, tile(kd, n), k_dst, dk_s.at[n], dk_r.at[me.head], me.par, me.core * 4 + n)

    for s in range(1, 4):
        for sub in range(2):
            step(0, s, sub)
            step(1, s, sub)

    def finish(sub):
        total = local_sum(me.z, sub_ylo(sub))
        for w in range(2):
            travel[w, 3, sub].wait_recv()
            total = total + ways[w][2][6 + sub].astype(F32)
        return total

    y_b[...] = finish(0).astype(BF)
    over = remote(y_b, y_in, one_s.at[5], one_r.at[5], me.across)
    over.start()
    wsum[...] = finish(1)
    over.wait()
    c_b[...] = (wsum[...] + y_in[...].astype(F32)).astype(BF)
    for n in range(16):
        push(
            me, c_b.at[pl.ds(n * 16, 16), :], c_in.at[me.core, me.ctx], c_s.at[n], c_r.at[me.core * N_CTX + me.ctx],
            n // N_CTX, n % N_CTX,
        )
    for n in range(16):
        landed(c_in.at[n // N_CTX, n % N_CTX], c_r.at[n])
    for half in range(2):
        total = c_in[half, 0].astype(F32)
        for i in range(1, N_CTX):
            total = total + c_in[half, i].astype(F32)
        wg[:, half * COLS : (half + 1) * COLS] = total

    for copies in started.values():
        for copy in copies:
            copy.wait_send()
    for n, (to, ctx) in enumerate(plane):
        pushed(me, w_src(to), w_s.at[n], to, ctx)
    for n in range(8):
        to, j = n // 4, n % 4
        pushed(me, k_src(j), k_s.at[n], to, me.core * 4 + j)
        pushed(me, wide(q, to, j), q_s.at[n], to, me.core * 4 + j)
        pushed(me, wide(g, to, j), g_s.at[n], to, me.core * 4 + j)
    for n, (to, p, jj) in enumerate(routes):
        pushed(me, v_src(p, jj), v_s.at[n], to, p * 4 + me.core * 2 + jj)
    for n in range(4):
        swaps[n].wait_send()
    for copy in travel.values():
        copy.wait_send()
    for n in range(16):
        pushed(me, c_b.at[pl.ds(n * 16, 16), :], c_s.at[n], n // N_CTX, n % N_CTX)
    for n in range(4):
        pushed(me, tile(vd, n), dv_s.at[n], v_core, me.core * 4 + n)
        pushed(me, tile(kd, n), dk_s.at[n], me.par, me.core * 4 + n)
        landed(dko.at[:, pl.ds(n * HEAD, HEAD)], dk_r.at[n])
    for i in range(N_CTX):
        pushed(me, home(oc, i), o_s.at[i], me.par, i)
        pushed(me, home(dqc, i), d_s.at[i], me.par, i)
    for n in range(8):
        dst = (pl.ds(n // 4 * HALF, HALF), pl.ds(n % 4 * GROUP * HEAD, GROUP * HEAD))
        landed(att.at[dst], o_r.at[n])
        landed(dqo.at[dst], d_r.at[n])


def run(q, g, k, x, w, lens, plc, tsel, bits):
    slab = (256, COLS)
    rows = (SEQ // 2, GROUP * HEAD)
    table = (2, N_CTX, SEQ // 2, HEAD)
    return pl.pallas_call(
        kernel,
        out_shape=[
            jax.ShapeDtypeStruct((TOK, D), BF),
            jax.ShapeDtypeStruct((TOK, D), BF),
            jax.ShapeDtypeStruct((TOK, KVW), BF),
            jax.ShapeDtypeStruct((16, KVW), F32),
        ],
        in_specs=[ANY] * 9,
        out_specs=[ANY] * 3 + [pl.BlockSpec(memory_space=pltpu.VMEM)],
        scratch_shapes=[
            vmem((2, N_Z, 256, COLS), BF), vmem((2, TOK, D), BF), vmem((2 * TOK, COLS), BF), vmem((2 * TOK, COLS), F32),
            vmem(rows, BF), vmem(rows, BF), vmem(rows, BF), vmem(rows, BF),
            vmem((PAD_ROWS, HEAD), BF), vmem((PAD_ROWS, HEAD), BF), vmem((2, HEAD, 1536), BF), vmem((2, HEAD, 1536), BF),
            vmem((2,) + lens.shape, I32), vmem((2,) + plc.shape, I32),
            vmem(bits.shape, I32), vmem((SEQ // 2, HEAD), F32), vmem(tsel.shape, I32), vmem((N_CTX * BLOCK, CAND * BLOCK), I32),
            vmem((16, WIN, GROUP * BLOCK), BF), vmem((16, SPAN, 2 * HEAD), BF),
            vmem(table, BF), vmem(table, BF), vmem(table, BF),
            vmem((2 * TOK, COLS), BF), vmem((SEQ // 2, HEAD), BF), vmem((SEQ // 2, HEAD), BF),
            vmem((8,) + slab, BF), vmem((8,) + slab, BF), vmem((8,) + slab, BF), vmem((8,) + slab, BF),
            vmem(slab, BF), vmem(slab, BF), vmem(slab, BF), vmem((2, N_CTX, 16, COLS), BF), vmem(slab, F32),
            dma(16), dma(16), dma(8), dma(8), dma(8), dma(8), dma(8), dma(8), dma(8), dma(8),
            dma(6), dma(6), dma(4 * SUBS), dma(4 * SUBS), dma(4 * SUBS), dma(4 * SUBS), dma(5),
            dma(4), dma(4), dma(8), dma(8), dma(8), dma(8), dma(4), dma(4), dma(4), dma(4),
            dma(8), dma(8), dma(8), dma(8), dma(16), dma(16),
        ],
        compiler_params=pltpu.CompilerParams(
            collective_id=0, has_side_effects=True, vmem_limit_bytes=60 * 2**20
        ),
        cost_estimate=pl.CostEstimate(flops=6 * 10**9, bytes_accessed=16 * 2**20, transcendentals=2 * 10**6),
        name="cycle",
    )(q, g, k, x, w, lens, plc, tsel, bits)


def move_kernel(*refs):
    for n in range(4):
        refs[4 + n][...] = refs[n][...]


def move(arrays):
    steps = 2
    specs = [pl.BlockSpec((a.shape[0] // steps, a.shape[1]), lambda i: (i, 0)) for a in arrays]
    return pl.pallas_call(
        move_kernel,
        grid=(steps,),
        out_shape=[jax.ShapeDtypeStruct(a.shape, a.dtype) for a in arrays],
        in_specs=specs,
        out_specs=specs,
        compiler_params=pltpu.CompilerParams(vmem_limit_bytes=60 * 2**20),
        name="move",
    )(*arrays)


def local(queries, key_vectors, activations, value_weight, attended_grad, doc_ids, shard_plan, round_bits):
    docs = jnp.arange(16, dtype=I32)
    starts = jnp.sum((doc_ids < docs[:, None]).astype(I32), axis=1)
    first = jnp.sum(jnp.where(doc_ids == docs[:, None], starts[:, None], 0), axis=0)
    earlier = (jnp.arange(SEQ, dtype=I32) - first).reshape(SEQ // BLOCK, BLOCK)
    lens = jnp.tile(earlier, (1, GROUP))
    blocks = jnp.arange(SEQ // BLOCK, dtype=I32)
    plan = shard_plan[0]
    place = jnp.sum(jnp.where(plan[:, None] == blocks[None, :], blocks[:, None], 0), axis=0)
    token = jnp.arange(SEQ, dtype=I32)
    token_place = jnp.sum(jnp.where(plan[:, None] == token[None, :] // BLOCK, blocks[:, None], 0), axis=0)
    plc = jnp.broadcast_to((token_place * BLOCK + token % BLOCK)[None, :], (8, SEQ))
    shape = (2, SEQ // BLOCK, CAND * BLOCK)
    core, key_block, col = [lax.broadcasted_iota(I32, shape, n) for n in range(3)]
    cand = col // BLOCK
    query_block = (key_block // 4 + cand // 2) * 4 + core * 2 + cand % 2
    ahead = query_block - key_block
    seen = (cand < 10) & (query_block < SEQ // BLOCK) & (ahead >= 0) & (ahead <= BAND // BLOCK)
    hit = query_block[..., None] == plan
    owner = jnp.sum(jnp.where(hit, blocks // 4, 0), axis=-1)
    step = (owner - (place // 4)[None, :, None]) % N_CTX
    tsel = jnp.where(seen, step, -1)
    bits = round_bits.transpose(0, 2, 1).reshape(N_CTX * 8, SEQ)
    outs = run(
        queries[0], attended_grad[0], key_vectors[0], activations[0], value_weight, lens, plc, tsel, bits
    )
    att, dqo, dko, wg = move(outs)
    return att[None], dqo[None], dko[None], wg


def solution(mesh):
    rows = P("dp", "ctx", None)
    every = P(("dp", "ctx"), None)
    return jax.shard_map(
        local,
        mesh=mesh,
        in_specs=(rows, rows, rows, every, rows, P("dp", None), P("dp", None), P()),
        out_specs=(rows, rows, rows, every),
        check_vma=False,
    )
```

time: 140 us -> 124 us (0.89)
  Pallas kernels: 129 us -> 117 us
  local copies, waits for them, and re-layouts: 7.28 us -> 1.41 us
  other arithmetic: 2.34 us -> 5.31 us
    pallas_call x3 -> x2, Pallas kernels: 129 us -> 117 us  [the longest x1 114 us: run(): pl.pallas_call(kernel, out_shape=[jax.ShapeDtypeStruct((TOK, D), BF), jax...]
    unnamed x8 -> x0, local copies, waits for them, and re-layouts: 5.89 us -> none
    reduce_sum x1 -> x3, other arithmetic: 0.75 us -> 2.79 us  [the longest x1 1.29 us: local(): owner = jnp.sum(jnp.where(hit, blocks // 4, 0), axis=-1)]
where the time goes in v3:
time: 124 us
  Pallas kernels  117 us (94%)
  other arithmetic  5.31 us (4%)
  local copies, waits for them, and re-layouts  1.41 us (1%)
    pallas_call x1, Pallas kernels, run(): pl.pallas_call(kernel, out_shape=[jax.ShapeDtypeStruct((TOK, D), BF), jax...  114 us
    pallas_call x1, Pallas kernels, move(): pl.pallas_call(move_kernel, grid=(steps,), out_shape=[jax.ShapeDtypeStruc...  2.65 us

profile of v3, /device:TPU:1, one launch (start us, length us, event | category | flops | bytes accessed | tf_op | source)
XLA Modules:
  0.0 124.2 jit_solution(13785322409654812815)
XLA Ops:
  0.7 0.8 convert_reduce_fusion
  1.5 0.7 select_reduce_fusion.3
  2.3 0.8 select_reduce_fusion.2
  3.0 0.7 select_reduce_fusion.1
  3.8 0.1 reduce_sum.49
  3.9 0.6 broadcast_in_dim.74.plc
  4.5 0.1 fusion.3
  4.6 1.3 %select_reduce_fusion = s32[2,32,384]{2,1,0:T(8,128)S(1)} fusion(s32[32]{0:T(128)S(1)} %fusion.24, s32[2,32,384]{2,1,0:T(8,128)S(1)} %fusion.3, s32[32]{0:T(128)} %bitcast.16), kind=kLoop, calls=%fused_computation | loop fusion | flops 2334720 | bytes 196864 | tf_op jit(solution)/shard_map/reduce_sum | solution.py:558
  5.9 0.8 fusion.5.tsel
  6.7 0.7 tile.9.lens
  7.4 114.1 %cycle.1 = (bf16[128,4096]{1,0:T(8,128)(2,1)}, bf16[128,4096]{1,0:T(8,128)(2,1)}, bf16[128,512]{1,0:T(8,128)(2,1)}, f32[16,512]{1,0:T(8,128)}) custom-call(bf16[128,4096]{1,0:T(8,128)(2,1)} %bitcast.17, bf16[128,4096]{1,0:T(8,128)(2,1)} %bitcast.18, bf16[128,512]{1,0:T(8,128)(2,1)} %bitcast.23, bf16[128,4096]{1,0:T(8,128)(2,1)} %bitcast.19, ...), custom_call_target="tpu_custom_call" | custom-call | flops 6000000000 | bytes 16777216 | tf_op jit(solution)/shard_map/cycle/pallas_call | solution.py:486
  121.5 2.6 %move.1 = (bf16[128,4096]{1,0:T(8,128)(2,1)}, bf16[128,4096]{1,0:T(8,128)(2,1)}, bf16[128,512]{1,0:T(8,128)(2,1)}, f32[16,512]{1,0:T(8,128)}) custom-call(bf16[128,4096]{1,0:T(8,128)(2,1)} %get-tuple-element.12.refs_0_, bf16[128,4096]{1,0:T(8,128)(2,1)} %get-tuple-element.13.refs_1_, bf16[128,512]{1,0:T(8,128)(2,1)} %get-tuple-element.14.refs_2_, ...), custom_call_target="tpu_custom_call" | custom-call | tf_op jit(solution)/shard_map/move/pallas_call | solution.py:528
  (11 shorter events, 0.1 us)

commit v4 on v3

--- a/solution.py
+++ b/solution.py
@@ -111,8 +111,8 @@
 
 
 def kernel(
-    q, g, k, x, w, lens, plc, tsel, bits, att, dqo, dko, wg,
-    wfull, xv, vbuf, vacc, qa, ga, oc, dqc, kpad, vpad, kt, vt, lensv, plcv, bitv, jit,
+    q, g, k, x, w, docs, plan, bits, att, dqo, dko, wg,
+    wfull, xv, vbuf, vacc, qa, ga, oc, dqc, kpad, vpad, kt, vt, docv, planv, planrow, firstv, bitv, jit,
     tsv, code, pst, kvb, away_t, own_t, part, dv_pair, kd, vd,
     up_b, dn_b, up_in, dn_in, y_b, y_in, c_b, c_in, wsum,
     w_s, w_r, q_s, q_r, g_s, g_r, k_s, k_r, v_s, v_r, one_s, one_r, up_s, up_r, dn_s, dn_r, loc,
@@ -141,15 +141,13 @@
         push(me, w_src(to), w_dst, w_s.at[n], w_r.at[me.core * N_CTX + me.ctx], to, ctx)
 
     own_x = pltpu.make_async_copy(x, xv.at[me.core], loc.at[0])
-    own_l = pltpu.make_async_copy(lens, lensv.at[me.core], loc.at[1])
-    own_p = pltpu.make_async_copy(plc, plcv.at[me.core], loc.at[2])
+    own_l = pltpu.make_async_copy(docs, docv.at[me.core], loc.at[1])
+    own_p = pltpu.make_async_copy(plan, planv.at[me.core], loc.at[2])
     far_x = remote(x, xv.at[me.core], one_s.at[0], one_r.at[0], me.partner)
-    far_l = remote(lens, lensv.at[me.core], one_s.at[1], one_r.at[1], me.partner)
-    far_p = remote(plc, plcv.at[me.core], one_s.at[2], one_r.at[2], me.partner)
-    own_t_sel = pltpu.make_async_copy(tsel.at[me.core], tsv.at[me.core], loc.at[4])
-    far_t_sel = remote(tsel.at[1 - me.core], tsv.at[me.core], one_s.at[4], one_r.at[4], me.partner)
+    far_l = remote(docs, docv.at[me.core], one_s.at[1], one_r.at[1], me.partner)
+    far_p = remote(plan, planv.at[me.core], one_s.at[2], one_r.at[2], me.partner)
     bits_in = pltpu.make_async_copy(bits, bitv, loc.at[3])
-    for copy in (own_x, far_x, own_l, far_l, own_p, far_p, own_t_sel, far_t_sel, bits_in):
+    for copy in (own_x, far_x, own_l, far_l, own_p, far_p, bits_in):
         copy.start()
 
     def k_src(j):
@@ -231,13 +229,49 @@
     key_row = lax.broadcasted_iota(I32, (WIN, GROUP * BLOCK), 0)
     lane = lax.broadcasted_iota(I32, (1, GROUP * BLOCK), 1) % BLOCK
 
+    def iota(shape, axis):
+        return lax.broadcasted_iota(I32, shape, axis)
+
+    def tables():
+        doc = docv[par]
+        first = jnp.zeros(doc.shape, I32)
+        for d in range(15):
+            size = jnp.sum(jnp.where(doc == d, 1, 0), axis=1, keepdims=True)
+            first = first + jnp.where(doc > d, size, 0)
+        first = jnp.broadcast_to(first, (SEQ // BLOCK, SEQ))
+        mine = iota(first.shape, 0) == iota(first.shape, 1) // BLOCK
+        same = iota((SEQ, GROUP * BLOCK), 0) % BLOCK == iota((SEQ, GROUP * BLOCK), 1) % BLOCK
+        same = jnp.where(same, 1.0, 0.0).astype(BF)
+        spread = []
+        for part in (first // BLOCK, first % BLOCK):
+            part = jnp.where(mine, part, 0).astype(F32).astype(BF)
+            spread.append(jnp.dot(part, same, preferred_element_type=F32).astype(I32))
+        firstv[...] = spread[0] * BLOCK + spread[1]
+
+        plan = planv[par]
+        block = iota((1, SEQ), 1) // BLOCK
+        key_block, col = iota(tsv.shape, 0), iota(tsv.shape, 1)
+        cand = col // BLOCK
+        query_block = (key_block // 4 + cand // 2) * 4 + core * 2 + cand % 2
+        place = jnp.zeros((1, SEQ), I32)
+        step = jnp.zeros(tsv.shape, I32)
+        for p in range(SEQ // BLOCK):
+            at = plan[:, p : p + 1]
+            place = place + jnp.where(block == at, p, 0)
+            step = step + jnp.where(query_block == at, p // 4, 0) - jnp.where(key_block == at, p // 4, 0)
+        step = jnp.where(step < 0, step + N_CTX, step)
+        ahead = query_block - key_block
+        seen = (cand < 10) & (query_block < SEQ // BLOCK) & (ahead >= 0) & (ahead <= BAND // BLOCK)
+        tsv[...] = jnp.where(seen, step, -1)
+        planrow[...] = place * BLOCK + iota((1, SEQ), 1) % BLOCK
+
     def scores(low, high):
         @pl.loop(low, high)
         def _(i):
             landed(qa.at[pl.ds(pl.multiple_of(i * HALF, HALF), HALF), :], q_r.at[i])
             for b in range(2):
                 block, rows = keys_of(i, b)
-                first = lane + BAND - lensv[par, pl.ds(block, 1), :]
+                first = firstv[pl.ds(block, 1), :] + (BAND - block * BLOCK)
                 allowed = (key_row >= first) & (key_row <= lane + BAND)
                 s = lax.dot_general(kpad[rows, :], stacked(qa, i, b), NT, preferred_element_type=F32)
                 s = jnp.where(allowed, s * (SCALE * LOG2E), NEG)
@@ -257,8 +291,9 @@
     for i in range(N_CTX):
         landed(kpad.at[pl.ds(BAND + i * TOK, TOK), :], k_r.at[i])
     transposed(kt, kpad)
-    for copy in (own_l, far_l, own_p, far_p, own_t_sel, far_t_sel):
+    for copy in (own_l, far_l, own_p, far_p):
         copy.wait()
+    tables()
     project((me.z + N_Z - 3) % N_Z)
     project((me.z + 3) % N_Z)
     scores(0, 3)
@@ -284,7 +319,7 @@
     for _ in range(3):
         parts.append(jitter.astype(BF))
         jitter = jitter - parts[-1].astype(F32)
-    at = plcv[par, 0:1, pl.ds(pl.multiple_of(core * (SEQ // 2), SEQ // 2), SEQ // 2)]
+    at = planrow[:, pl.ds(pl.multiple_of(core * (SEQ // 2), SEQ // 2), SEQ // 2)]
     there = lax.broadcasted_iota(I32, (SEQ, SEQ // 2), 0) == at
     moved = jnp.dot(
         jnp.concatenate(parts, axis=0), jnp.where(there, 1.0, 0.0).astype(BF), preferred_element_type=F32
@@ -333,7 +368,7 @@
                 row = EDGE + BAND + (m - c // 2 * 4 - core * 2 - b) * BLOCK
                 pieces.append(kvb[i * 2 + b, pl.ds(pl.multiple_of(row, BLOCK), BLOCK), :])
             pieces += pieces[0:2]
-            step = tsv[par, pl.ds(tile_at * 4 + m, 1), :]
+            step = tsv[pl.ds(tile_at * 4 + m, 1), :]
             pick = jnp.where(code[...] == step, 1.0, 0.0).astype(BF)
             sums = jnp.dot(pick, jnp.concatenate(pieces, axis=0), preferred_element_type=F32).astype(BF)
             dst = pl.ds(pl.multiple_of(n * TOK + m * BLOCK, BLOCK), BLOCK)
@@ -479,7 +514,7 @@
         landed(dqo.at[dst], d_r.at[n])
 
 
-def run(q, g, k, x, w, lens, plc, tsel, bits):
+def run(q, g, k, x, w, docs, plan, bits):
     slab = (256, COLS)
     rows = (SEQ // 2, GROUP * HEAD)
     table = (2, N_CTX, SEQ // 2, HEAD)
@@ -491,14 +526,15 @@
             jax.ShapeDtypeStruct((TOK, KVW), BF),
             jax.ShapeDtypeStruct((16, KVW), F32),
         ],
-        in_specs=[ANY] * 9,
+        in_specs=[ANY] * 8,
         out_specs=[ANY] * 3 + [pl.BlockSpec(memory_space=pltpu.VMEM)],
         scratch_shapes=[
             vmem((2, N_Z, 256, COLS), BF), vmem((2, TOK, D), BF), vmem((2 * TOK, COLS), BF), vmem((2 * TOK, COLS), F32),
             vmem(rows, BF), vmem(rows, BF), vmem(rows, BF), vmem(rows, BF),
             vmem((PAD_ROWS, HEAD), BF), vmem((PAD_ROWS, HEAD), BF), vmem((2, HEAD, 1536), BF), vmem((2, HEAD, 1536), BF),
-            vmem((2,) + lens.shape, I32), vmem((2,) + plc.shape, I32),
-            vmem(bits.shape, I32), vmem((SEQ // 2, HEAD), F32), vmem(tsel.shape, I32), vmem((N_CTX * BLOCK, CAND * BLOCK), I32),
+            vmem((2,) + docs.shape, I32), vmem((2,) + plan.shape, I32), vmem(docs.shape, I32),
+            vmem((SEQ // BLOCK, GROUP * BLOCK), I32),
+            vmem(bits.shape, I32), vmem((SEQ // 2, HEAD), F32), vmem((SEQ // BLOCK, CAND * BLOCK), I32), vmem((N_CTX * BLOCK, CAND * BLOCK), I32),
             vmem((16, WIN, GROUP * BLOCK), BF), vmem((16, SPAN, 2 * HEAD), BF),
             vmem(table, BF), vmem(table, BF), vmem(table, BF),
             vmem((2 * TOK, COLS), BF), vmem((SEQ // 2, HEAD), BF), vmem((SEQ // 2, HEAD), BF),
@@ -514,7 +550,7 @@
         ),
         cost_estimate=pl.CostEstimate(flops=6 * 10**9, bytes_accessed=16 * 2**20, transcendentals=2 * 10**6),
         name="cycle",
-    )(q, g, k, x, w, lens, plc, tsel, bits)
+    )(q, g, k, x, w, docs, plan, bits)
 
 
 def move_kernel(*refs):
@@ -537,30 +573,9 @@
 
 
 def local(queries, key_vectors, activations, value_weight, attended_grad, doc_ids, shard_plan, round_bits):
-    docs = jnp.arange(16, dtype=I32)
-    starts = jnp.sum((doc_ids < docs[:, None]).astype(I32), axis=1)
-    first = jnp.sum(jnp.where(doc_ids == docs[:, None], starts[:, None], 0), axis=0)
-    earlier = (jnp.arange(SEQ, dtype=I32) - first).reshape(SEQ // BLOCK, BLOCK)
-    lens = jnp.tile(earlier, (1, GROUP))
-    blocks = jnp.arange(SEQ // BLOCK, dtype=I32)
-    plan = shard_plan[0]
-    place = jnp.sum(jnp.where(plan[:, None] == blocks[None, :], blocks[:, None], 0), axis=0)
-    token = jnp.arange(SEQ, dtype=I32)
-    token_place = jnp.sum(jnp.where(plan[:, None] == token[None, :] // BLOCK, blocks[:, None], 0), axis=0)
-    plc = jnp.broadcast_to((token_place * BLOCK + token % BLOCK)[None, :], (8, SEQ))
-    shape = (2, SEQ // BLOCK, CAND * BLOCK)
-    core, key_block, col = [lax.broadcasted_iota(I32, shape, n) for n in range(3)]
-    cand = col // BLOCK
-    query_block = (key_block // 4 + cand // 2) * 4 + core * 2 + cand % 2
-    ahead = query_block - key_block
-    seen = (cand < 10) & (query_block < SEQ // BLOCK) & (ahead >= 0) & (ahead <= BAND // BLOCK)
-    hit = query_block[..., None] == plan
-    owner = jnp.sum(jnp.where(hit, blocks // 4, 0), axis=-1)
-    step = (owner - (place // 4)[None, :, None]) % N_CTX
-    tsel = jnp.where(seen, step, -1)
     bits = round_bits.transpose(0, 2, 1).reshape(N_CTX * 8, SEQ)
     outs = run(
-        queries[0], attended_grad[0], key_vectors[0], activations[0], value_weight, lens, plc, tsel, bits
+        queries[0], attended_grad[0], key_vectors[0], activations[0], value_weight, doc_ids, shard_plan, bits
     )
     att, dqo, dko, wg = move(outs)
     return att[None], dqo[None], dko[None], wg

time: 124 us -> 118 us (0.952)
  other arithmetic: 5.31 us -> 0 us
  local copies, waits for them, and re-layouts: 1.41 us -> 0 us
    reduce_sum x5 -> x0, other arithmetic: 4.37 us -> none  [the longest x1 1.29 us: local(): owner = jnp.sum(jnp.where(hit, blocks // 4, 0), axis=-1)]
where the time goes in v4:
time: 118 us
  Pallas kernels  117 us (99%)
    pallas_call x1, Pallas kernels, run(): pl.pallas_call(kernel, out_shape=[jax.ShapeDtypeStruct((TOK, D), BF), jax...  115 us
    pallas_call x1, Pallas kernels, move(): pl.pallas_call(move_kernel, grid=(steps,), out_shape=[jax.ShapeDtypeStruc...  2.65 us

profile of v4, /device:TPU:1, one launch (start us, length us, event | category | flops | bytes accessed | tf_op | source)
XLA Modules:
  0.0 117.9 jit_solution(4357634530332717718)
XLA Ops:
  0.6 114.6 %cycle.1 = (bf16[128,4096]{1,0:T(8,128)(2,1)}, bf16[128,4096]{1,0:T(8,128)(2,1)}, bf16[128,512]{1,0:T(8,128)(2,1)}, f32[16,512]{1,0:T(8,128)}) custom-call(bf16[128,4096]{1,0:T(8,128)(2,1)} %bitcast.10, bf16[128,4096]{1,0:T(8,128)(2,1)} %bitcast.11, bf16[128,512]{1,0:T(8,128)(2,1)} %bitcast.16, bf16[128,4096]{1,0:T(8,128)(2,1)} %bitcast.12, ...), custom_call_target="tpu_custom_call" | custom-call | flops 6000000000 | bytes 16777216 | tf_op jit(solution)/shard_map/cycle/pallas_call | solution.py:521
  115.2 2.6 %move.1 = (bf16[128,4096]{1,0:T(8,128)(2,1)}, bf16[128,4096]{1,0:T(8,128)(2,1)}, bf16[128,512]{1,0:T(8,128)(2,1)}, f32[16,512]{1,0:T(8,128)}) custom-call(bf16[128,4096]{1,0:T(8,128)(2,1)} %get-tuple-element.12.refs_0_, bf16[128,4096]{1,0:T(8,128)(2,1)} %get-tuple-element.13.refs_1_, bf16[128,512]{1,0:T(8,128)(2,1)} %get-tuple-element.14.refs_2_, ...), custom_call_target="tpu_custom_call" | custom-call | tf_op jit(solution)/shard_map/move/pallas_call | solution.py:564

commit v5 on v4

--- a/solution.py
+++ b/solution.py
@@ -60,26 +60,30 @@
         self.par = self.ctx // 4
         self.head = self.ctx % 4
         self.partner = (self.base + 1 - self.core, self.ctx)
-        self.across = (self.dp + 16 - 32 * self.ylo, self.ctx)
         self.up = (self.ylo * 16 + (self.z + 1) % N_Z * 2 + self.core, self.ctx)
         self.down = (self.ylo * 16 + (self.z + N_Z - 1) % N_Z * 2 + self.core, self.ctx)
 
+    def over_there(self, core, ctx):
+        return (self.base + 16 - 32 * self.ylo + core, jnp.int32(ctx))
+
     def is_me(self, core, ctx):
         return (self.core == core) & (self.ctx == ctx)
 
 
 def greet(me):
     barrier = pltpu.get_barrier_semaphore()
-    for core in range(2):
-        for ctx in range(N_CTX):
-
-            @pl.when(jnp.logical_not(me.is_me(core, ctx)))
-            def _(core=core, ctx=ctx):
-                pl.semaphore_signal(barrier, inc=1, device_id=(me.base + core, jnp.int32(ctx)), device_id_type=MESH)
-
-    for other in (me.across, me.up, me.down):
+    for ylo in range(2):
+        for core in range(2):
+            for ctx in range(N_CTX):
+
+                @pl.when(jnp.logical_not((me.ylo == ylo) & me.is_me(core, ctx)))
+                def _(ylo=ylo, core=core, ctx=ctx):
+                    to = (ylo * 16 + me.z * 2 + core, jnp.int32(ctx))
+                    pl.semaphore_signal(barrier, inc=1, device_id=to, device_id_type=MESH)
+
+    for other in (me.up, me.down):
         pl.semaphore_signal(barrier, inc=1, device_id=other, device_id_type=MESH)
-    pl.semaphore_wait(barrier, 2 * N_CTX + 2)
+    pl.semaphore_wait(barrier, 4 * N_CTX + 1)
 
 
 def remote(src, dst, ssem, rsem, device):
@@ -114,7 +118,7 @@
     q, g, k, x, w, docs, plan, bits, att, dqo, dko, wg,
     wfull, xv, vbuf, vacc, qa, ga, oc, dqc, kpad, vpad, kt, vt, docv, planv, planrow, firstv, bitv, jit,
     tsv, code, pst, kvb, away_t, own_t, part, dv_pair, kd, vd,
-    up_b, dn_b, up_in, dn_in, y_b, y_in, c_b, c_in, wsum,
+    up_b, dn_b, up_in, dn_in, c_b, c_in,
     w_s, w_r, q_s, q_r, g_s, g_r, k_s, k_r, v_s, v_r, one_s, one_r, up_s, up_r, dn_s, dn_r, loc,
     sw_s, sw_r, o_s, o_r, d_s, d_r, dk_s, dk_r, dv_s, dv_r, ru_s, ru_r, rd_s, rd_r, c_s, c_r,
 ):
@@ -139,6 +143,8 @@
     w_dst = wfull.at[me.ylo, me.z, pl.ds(row, 16), :]
     for n, (to, ctx) in enumerate(plane):
         push(me, w_src(to), w_dst, w_s.at[n], w_r.at[me.core * N_CTX + me.ctx], to, ctx)
+    for n, (to, ctx) in enumerate(plane):
+        remote(w_src(to), w_dst, w_s.at[16 + n], w_r.at[16 + me.core * N_CTX + me.ctx], me.over_there(to, ctx)).start()
 
     own_x = pltpu.make_async_copy(x, xv.at[me.core], loc.at[0])
     own_l = pltpu.make_async_copy(docs, docv.at[me.core], loc.at[1])
@@ -164,10 +170,6 @@
         push(me, k_src(j), kpad.at[pl.ds(spot, TOK), :], k_s.at[n], k_r.at[me.ctx], to, me.core * 4 + j)
     for n in range(16):
         landed(wfull.at[me.ylo, me.z, pl.ds(n * 16, 16), :], w_r.at[n])
-    mine = wfull.at[me.ylo, me.z]
-    over = remote(mine, mine, one_s.at[3], one_r.at[3], me.across)
-    over.start()
-
     def piece(z, sub):
         ylo = me.ylo if sub < SUBS // 2 else 1 - me.ylo
         return wfull.at[ylo, z, pl.ds(sub % (SUBS // 2) * SUB_ROWS, SUB_ROWS), :]
@@ -197,7 +199,8 @@
         push(me, wide(g, to, j), ga.at[pl.ds(half_spot, HALF), :], g_s.at[n], g_r.at[me.ctx], to, me.core * 4 + j)
     own_x.wait()
     far_x.wait()
-    over.wait()
+    for n in range(16):
+        landed(wfull.at[1 - me.ylo, me.z, pl.ds(n * 16, 16), :], w_r.at[16 + n])
     for sub in range(SUBS // 2, SUBS):
         go(0, sub)
 
@@ -462,24 +465,26 @@
         for w in range(2):
             travel[w, 3, sub].wait_recv()
             total = total + ways[w][2][6 + sub].astype(F32)
-        return total
-
-    y_b[...] = finish(0).astype(BF)
-    over = remote(y_b, y_in, one_s.at[5], one_r.at[5], me.across)
-    over.start()
-    wsum[...] = finish(1)
-    over.wait()
-    c_b[...] = (wsum[...] + y_in[...].astype(F32)).astype(BF)
+        c_b[sub] = total.astype(BF)
+
+    def c_src(sub, n):
+        return c_b.at[sub, pl.ds(n * 16, 16), :]
+
+    far_in, near_in = c_in.at[me.core, N_CTX + me.ctx], c_in.at[me.core, me.ctx]
+    mine = me.core * N_CTX + me.ctx
+    finish(0)
+    for n, (to, ctx) in enumerate(plane):
+        remote(c_src(0, n), far_in, c_s.at[16 + n], c_r.at[16 + mine], me.over_there(to, ctx)).start()
+    finish(1)
+    for n, (to, ctx) in enumerate(plane):
+        push(me, c_src(1, n), near_in, c_s.at[n], c_r.at[mine], to, ctx)
     for n in range(16):
-        push(
-            me, c_b.at[pl.ds(n * 16, 16), :], c_in.at[me.core, me.ctx], c_s.at[n], c_r.at[me.core * N_CTX + me.ctx],
-            n // N_CTX, n % N_CTX,
-        )
+        landed(c_in.at[n // N_CTX, N_CTX + n % N_CTX], c_r.at[16 + n])
     for n in range(16):
         landed(c_in.at[n // N_CTX, n % N_CTX], c_r.at[n])
     for half in range(2):
         total = c_in[half, 0].astype(F32)
-        for i in range(1, N_CTX):
+        for i in range(1, 2 * N_CTX):
             total = total + c_in[half, i].astype(F32)
         wg[:, half * COLS : (half + 1) * COLS] = total
 
@@ -488,6 +493,7 @@
             copy.wait_send()
     for n, (to, ctx) in enumerate(plane):
         pushed(me, w_src(to), w_s.at[n], to, ctx)
+        remote(w_src(to), w_dst, w_s.at[16 + n], w_r.at[16 + n], me.over_there(to, ctx)).wait_send()
     for n in range(8):
         to, j = n // 4, n % 4
         pushed(me, k_src(j), k_s.at[n], to, me.core * 4 + j)
@@ -499,8 +505,9 @@
         swaps[n].wait_send()
     for copy in travel.values():
         copy.wait_send()
-    for n in range(16):
-        pushed(me, c_b.at[pl.ds(n * 16, 16), :], c_s.at[n], n // N_CTX, n % N_CTX)
+    for n, (to, ctx) in enumerate(plane):
+        pushed(me, c_src(1, n), c_s.at[n], to, ctx)
+        remote(c_src(0, n), far_in, c_s.at[16 + n], c_r.at[16 + n], me.over_there(to, ctx)).wait_send()
     for n in range(4):
         pushed(me, tile(vd, n), dv_s.at[n], v_core, me.core * 4 + n)
         pushed(me, tile(kd, n), dk_s.at[n], me.par, me.core * 4 + n)
@@ -539,11 +546,11 @@
             vmem(table, BF), vmem(table, BF), vmem(table, BF),
             vmem((2 * TOK, COLS), BF), vmem((SEQ // 2, HEAD), BF), vmem((SEQ // 2, HEAD), BF),
             vmem((8,) + slab, BF), vmem((8,) + slab, BF), vmem((8,) + slab, BF), vmem((8,) + slab, BF),
-            vmem(slab, BF), vmem(slab, BF), vmem(slab, BF), vmem((2, N_CTX, 16, COLS), BF), vmem(slab, F32),
-            dma(16), dma(16), dma(8), dma(8), dma(8), dma(8), dma(8), dma(8), dma(8), dma(8),
+            vmem((2,) + slab, BF), vmem((2, 2 * N_CTX, 16, COLS), BF),
+            dma(32), dma(32), dma(8), dma(8), dma(8), dma(8), dma(8), dma(8), dma(8), dma(8),
             dma(6), dma(6), dma(4 * SUBS), dma(4 * SUBS), dma(4 * SUBS), dma(4 * SUBS), dma(5),
             dma(4), dma(4), dma(8), dma(8), dma(8), dma(8), dma(4), dma(4), dma(4), dma(4),
-            dma(8), dma(8), dma(8), dma(8), dma(16), dma(16),
+            dma(8), dma(8), dma(8), dma(8), dma(32), dma(32),
         ],
         compiler_params=pltpu.CompilerParams(
             collective_id=0, has_side_effects=True, vmem_limit_bytes=60 * 2**20

time: 118 us -> 108 us (0.915)
  Pallas kernels: 117 us -> 107 us
    pallas_call x1, Pallas kernels: 115 us -> 104 us  [run(): pl.pallas_call(kernel, out_shape=[jax.ShapeDtypeStruct((TOK, D), BF), jax...]
where the time goes in v5:
time: 108 us
  Pallas kernels  107 us (99%)
    pallas_call x1, Pallas kernels, run(): pl.pallas_call(kernel, out_shape=[jax.ShapeDtypeStruct((TOK, D), BF), jax...  104 us
    pallas_call x1, Pallas kernels, move(): pl.pallas_call(move_kernel, grid=(steps,), out_shape=[jax.ShapeDtypeStruc...  2.65 us

profile of v5, /device:TPU:1, one launch (start us, length us, event | category | flops | bytes accessed | tf_op | source)
XLA Modules:
  0.0 107.5 jit_solution(10536842721215819788)
XLA Ops:
  0.6 104.2 %cycle.1 = (bf16[128,4096]{1,0:T(8,128)(2,1)}, bf16[128,4096]{1,0:T(8,128)(2,1)}, bf16[128,512]{1,0:T(8,128)(2,1)}, f32[16,512]{1,0:T(8,128)}) custom-call(bf16[128,4096]{1,0:T(8,128)(2,1)} %bitcast.10, bf16[128,4096]{1,0:T(8,128)(2,1)} %bitcast.11, bf16[128,512]{1,0:T(8,128)(2,1)} %bitcast.16, bf16[128,4096]{1,0:T(8,128)(2,1)} %bitcast.12, ...), custom_call_target="tpu_custom_call" | custom-call | flops 6000000000 | bytes 16777216 | tf_op jit(solution)/shard_map/cycle/pallas_call | solution.py:528
  104.9 2.6 %move.1 = (bf16[128,4096]{1,0:T(8,128)(2,1)}, bf16[128,4096]{1,0:T(8,128)(2,1)}, bf16[128,512]{1,0:T(8,128)(2,1)}, f32[16,512]{1,0:T(8,128)}) custom-call(bf16[128,4096]{1,0:T(8,128)(2,1)} %get-tuple-element.12.refs_0_, bf16[128,4096]{1,0:T(8,128)(2,1)} %get-tuple-element.13.refs_1_, bf16[128,512]{1,0:T(8,128)(2,1)} %get-tuple-element.14.refs_2_, ...), custom_call_target="tpu_custom_call" | custom-call | tf_op jit(solution)/shard_map/move/pallas_call | solution.py:571

commit v6 on v5

--- a/solution.py
+++ b/solution.py
@@ -156,17 +156,21 @@
     for copy in (own_x, far_x, own_l, far_l, own_p, far_p, bits_in):
         copy.start()
 
+    def turned(n):
+        return (n + me.ctx) % N_CTX
+
     def k_src(j):
-        return k.at[:, pl.ds(j * HEAD, HEAD)]
+        return k.at[:, pl.ds(pl.multiple_of(j * HEAD, HEAD), HEAD)]
 
     def wide(ref, core, j):
-        return ref.at[pl.ds(core * HALF, HALF), pl.ds(j * GROUP * HEAD, GROUP * HEAD)]
+        cols = pl.ds(pl.multiple_of(j * GROUP * HEAD, HEAD), GROUP * HEAD)
+        return ref.at[pl.ds(pl.multiple_of(core * HALF, HALF), HALF), cols]
 
     spot = pl.multiple_of(BAND + me.ctx * TOK, TOK)
     half_spot = pl.multiple_of(me.ctx * HALF, HALF)
 
     for n in range(8):
-        to, j = n // 4, n % 4
+        to, j = turned(n) // 4, turned(n) % 4
         push(me, k_src(j), kpad.at[pl.ds(spot, TOK), :], k_s.at[n], k_r.at[me.ctx], to, me.core * 4 + j)
     for n in range(16):
         landed(wfull.at[me.ylo, me.z, pl.ds(n * 16, 16), :], w_r.at[n])
@@ -191,12 +195,6 @@
 
     for sub in range(SUBS // 2):
         go(0, sub)
-    for n in range(8):
-        to, j = n // 4, n % 4
-        push(me, wide(q, to, j), qa.at[pl.ds(half_spot, HALF), :], q_s.at[n], q_r.at[me.ctx], to, me.core * 4 + j)
-    for n in range(8):
-        to, j = n // 4, n % 4
-        push(me, wide(g, to, j), ga.at[pl.ds(half_spot, HALF), :], g_s.at[n], g_r.at[me.ctx], to, me.core * 4 + j)
     own_x.wait()
     far_x.wait()
     for n in range(16):
@@ -204,6 +202,12 @@
     for sub in range(SUBS // 2, SUBS):
         go(0, sub)
 
+    for n in range(8):
+        to, j = turned(n) // 4, turned(n) % 4
+        push(me, wide(q, to, j), qa.at[pl.ds(half_spot, HALF), :], q_s.at[n], q_r.at[me.ctx], to, me.core * 4 + j)
+    for n in range(8):
+        to, j = turned(n) // 4, turned(n) % 4
+        push(me, wide(g, to, j), ga.at[pl.ds(half_spot, HALF), :], g_s.at[n], g_r.at[me.ctx], to, me.core * 4 + j)
     def project(z):
         for ylo in range(2):
             col = pl.multiple_of(ylo * 2048 + z * 256, 256)
@@ -282,12 +286,19 @@
                 prob = weight * (1.0 / jnp.sum(weight, axis=0, keepdims=True))
                 pst[i * 2 + b] = prob.astype(BF)
 
+    def order(s, sub):
+        up, dn = started[s - 1, sub]
+        return (up, dn) if sub % 2 == 0 else (dn, up)
+
     for s in range(1, 4):
         for sub in range(SUBS):
-            up, dn = started[s - 1, sub]
-            up.wait_recv()
-            dn.wait_recv()
-            go(s, sub)
+            started[s, sub] = ring(s, sub)
+            first, second = started[s - 1, sub] if s < 3 else order(s, sub)
+            first.wait_recv()
+            started[s, sub][0].start()
+            second.wait_recv()
+            for copy in started[s, sub][1:]:
+                copy.start()
         project((me.z + N_Z - s + 1) % N_Z)
         if s > 1:
             project((me.z + s - 1) % N_Z)
@@ -450,15 +461,16 @@
     step(0, 0, 0)
     step(1, 0, 1)
 
-    for i in range(N_CTX):
-        push(me, home(dqc, i), out_wide(dqo, me.head), d_s.at[i], d_r.at[me.core * 4 + me.head], me.par, i)
-    for n in range(4):
-        push(me, tile(kd, n), k_dst, dk_s.at[n], dk_r.at[me.head], me.par, me.core * 4 + n)
 
     for s in range(1, 4):
         for sub in range(2):
             step(0, s, sub)
             step(1, s, sub)
+        if s == 1:
+            for i in range(N_CTX):
+                push(me, home(dqc, turned(i)), out_wide(dqo, me.head), d_s.at[i], d_r.at[me.core * 4 + me.head], me.par, turned(i))
+            for n in range(4):
+                push(me, tile(kd, n), k_dst, dk_s.at[n], dk_r.at[me.head], me.par, me.core * 4 + n)
 
     def finish(sub):
         total = local_sum(me.z, sub_ylo(sub))
@@ -495,7 +507,7 @@
         pushed(me, w_src(to), w_s.at[n], to, ctx)
         remote(w_src(to), w_dst, w_s.at[16 + n], w_r.at[16 + n], me.over_there(to, ctx)).wait_send()
     for n in range(8):
-        to, j = n // 4, n % 4
+        to, j = turned(n) // 4, turned(n) % 4
         pushed(me, k_src(j), k_s.at[n], to, me.core * 4 + j)
         pushed(me, wide(q, to, j), q_s.at[n], to, me.core * 4 + j)
         pushed(me, wide(g, to, j), g_s.at[n], to, me.core * 4 + j)
@@ -514,7 +526,7 @@
         landed(dko.at[:, pl.ds(n * HEAD, HEAD)], dk_r.at[n])
     for i in range(N_CTX):
         pushed(me, home(oc, i), o_s.at[i], me.par, i)
-        pushed(me, home(dqc, i), d_s.at[i], me.par, i)
+        pushed(me, home(dqc, turned(i)), d_s.at[i], me.par, turned(i))
     for n in range(8):
         dst = (pl.ds(n // 4 * HALF, HALF), pl.ds(n % 4 * GROUP * HEAD, GROUP * HEAD))
         landed(att.at[dst], o_r.at[n])

time: 108 us -> 108 us (level)
  no operation moved by 1% of the time
where the time goes in v6:
time: 108 us
  Pallas kernels  107 us (99%)
    pallas_call x1, Pallas kernels, run(): pl.pallas_call(kernel, out_shape=[jax.ShapeDtypeStruct((TOK, D), BF), jax...  104 us
    pallas_call x1, Pallas kernels, move(): pl.pallas_call(move_kernel, grid=(steps,), out_shape=[jax.ShapeDtypeStruc...  2.65 us

profile of v6, /device:TPU:1, one launch (start us, length us, event | category | flops | bytes accessed | tf_op | source)
XLA Modules:
  0.0 107.8 jit_solution(15895657808899671770)
XLA Ops:
  0.6 104.5 %cycle.1 = (bf16[128,4096]{1,0:T(8,128)(2,1)}, bf16[128,4096]{1,0:T(8,128)(2,1)}, bf16[128,512]{1,0:T(8,128)(2,1)}, f32[16,512]{1,0:T(8,128)}) custom-call(bf16[128,4096]{1,0:T(8,128)(2,1)} %bitcast.10, bf16[128,4096]{1,0:T(8,128)(2,1)} %bitcast.11, bf16[128,512]{1,0:T(8,128)(2,1)} %bitcast.16, bf16[128,4096]{1,0:T(8,128)(2,1)} %bitcast.12, ...), custom_call_target="tpu_custom_call" | custom-call | flops 6000000000 | bytes 16777216 | tf_op jit(solution)/shard_map/cycle/pallas_call | solution.py:540
  105.1 2.6 %move.1 = (bf16[128,4096]{1,0:T(8,128)(2,1)}, bf16[128,4096]{1,0:T(8,128)(2,1)}, bf16[128,512]{1,0:T(8,128)(2,1)}, f32[16,512]{1,0:T(8,128)}) custom-call(bf16[128,4096]{1,0:T(8,128)(2,1)} %get-tuple-element.12.refs_0_, bf16[128,4096]{1,0:T(8,128)(2,1)} %get-tuple-element.13.refs_1_, bf16[128,512]{1,0:T(8,128)(2,1)} %get-tuple-element.14.refs_2_, ...), custom_call_target="tpu_custom_call" | custom-call | tf_op jit(solution)/shard_map/move/pallas_call | solution.py:583
